TPU v7x, 256 devices: a whole 4x4x8 slice. The times are simulated.
256 devices in a mesh: depth: 2 (over core), row: 16 (over x, y), col: 8 (over z).
Axes of the slice: x: 4, y: 4, z: 8, core: 2. Of those that a mesh axis runs over, the one named last changes fastest.
Arguments:
- rhs: float32 [2, 6, 16384, 1024], P(None, None, ('row', 'col'), 'depth'), may hold values from -6 to 6
- panels: bfloat16 [2, 2, 6, 16384, 512], P(None, None, 'depth', ('row', 'col')), may hold values from -0.1875 to 0.1875
- inverses: bfloat16 [2, 2, 512, 512], replicated, as said below
Outputs:
- result: float32 [2, 6, 16384, 1024], P(None, None, ('row', 'col'), 'depth')
Inputs may be any that keep to these rules, and one draw needn't show every extreme that they name: Each inverses[s] is a lower triangular complex block, nonzero on its diagonal.
All inputs are finite; a program needn't handle non-finite values.
Results may differ from a plain program's by a relative error of at most 0.0046.
Values may be sent and summed in bfloat16 or wider, within the bound.
No kernel may reach another device: no remote copies, remote signals or barrier semaphores. Data moves between devices by JAX's collectives and lax.ppermute only.
A program may use at most 128 MiB of HBM per device.

v0:
```python
import jax
import jax.numpy as jnp
from jax import lax
from jax.sharding import PartitionSpec as P


def from_root(block, axis, holder):
    block = jnp.where(lax.axis_index(axis) == holder, block, jnp.zeros_like(block))
    return lax.psum(block, axis)


def complex_dot(left_real, left_imag, right_real, right_imag):
    real_part = jnp.dot(left_real, right_real, preferred_element_type=jnp.float32) - jnp.dot(
        left_imag, right_imag, preferred_element_type=jnp.float32
    )
    imag_part = jnp.dot(left_real, right_imag, preferred_element_type=jnp.float32) + jnp.dot(
        left_imag, right_real, preferred_element_type=jnp.float32
    )
    return jnp.stack([real_part, imag_part])


def per_device(rhs, panels, inverses):
    members = lax.axis_size(("row", "col"))
    position = lax.axis_index(("row", "col"))
    col_count = lax.axis_size("col")
    piece_rows = rhs.shape[2]
    rhs_cols = rhs.shape[3]
    cycles_here = rhs.shape[1]
    block_size = inverses.shape[-1]
    per_block = block_size // piece_rows
    step_count = inverses.shape[0]
    cycle_ids = jnp.arange(cycles_here, dtype=jnp.int32)[:, None]
    inner_ids = jnp.arange(piece_rows, dtype=jnp.int32)[None, :]
    global_rows = (cycle_ids * members + position) * piece_rows + inner_ids
    state = rhs
    solutions = []
    for step_index in range(step_count):
        own_rows = state[:, 0].astype(jnp.bfloat16)
        owner = (position >= step_index * per_block) & (position < (step_index + 1) * per_block)
        offset_piece = jnp.clip(position - step_index * per_block, 0, per_block - 1) * piece_rows
        gathered = lax.all_gather(own_rows, "col", axis=1, tiled=True)
        first_piece = step_index * per_block
        root_row = first_piece // col_count
        offset_cols = first_piece % col_count * piece_rows
        block_rhs = gathered[:, offset_cols : offset_cols + block_size]
        whole_rhs = from_root(block_rhs, "row", root_row)
        solved = complex_dot(
            inverses[step_index, 0], inverses[step_index, 1], whole_rhs[0], whole_rhs[1]
        )
        solutions.append((owner, offset_piece, solved))
        solved_half = solved.astype(jnp.bfloat16)
        panel_part = lax.all_gather(panels[step_index], "depth", axis=1, tiled=True)
        count = panel_part.shape[1]
        flat_real = panel_part[0].reshape(count * piece_rows, block_size)
        flat_imag = panel_part[1].reshape(count * piece_rows, block_size)
        update = complex_dot(flat_real, flat_imag, solved_half[0], solved_half[1])
        update = update.reshape(2, count, piece_rows, rhs_cols)
        keep_mask = global_rows >= (step_index + 1) * block_size
        state = state - jnp.where(keep_mask[None, :, :, None], update, jnp.zeros_like(update))
    first_rows = state[:, 0]
    for owner, offset_piece, solved in solutions:
        part_rows = lax.dynamic_slice_in_dim(solved, offset_piece, piece_rows, 1)
        first_rows = jnp.where(owner, part_rows, first_rows)
    return state.at[:, 0].set(first_rows)


def solution(mesh):
    return jax.shard_map(
        per_device,
        mesh=mesh,
        in_specs=(
            P(None, None, ("row", "col"), "depth"),
            P(None, None, "depth", ("row", "col"), None),
            P(),
        ),
        out_specs=P(None, None, ("row", "col"), "depth"),
        check_vma=False,
    )
```

profile of v0, /device:TPU:1, one launch (start us, length us, event | category | flops | bytes accessed | tf_op | source)
XLA Modules:
  0.0 414.4 jit_solution(1384651309024430890)
XLA Ops:
  6.5 2.4 copy.12
  9.7 2.6 fusion.41
  12.4 44.7 %all-gather.9.cloned.1.call-done = bf16[2,1,1024,512]{2,3,0,1:T(8,128)(2,1)} async-done(((bf16[2,1,128,512]{2,3,0,1:T(8,128)(2,1)}), bf16[2,1,1024,512]{2,3,0,1:T(8,128)(2,1)}) %all-gather.9.cloned.1.call-update) | async-done | bytes 2097168 | tf_op jit(solution)/shard_map/all_gather | solution.py:41
  57.2 2.3 slice_select_fusion.1
  59.6 18.2 %all-gather.11.cloned.1.call-done = bf16[1,2,6,128,512]{4,3,2,1,0:T(8,128)(2,1)} async-done(((bf16[1,2,3,128,512]{4,3,2,1,0:T(8,128)(2,1)}), bf16[1,2,6,128,512]{4,3,2,1,0:T(8,128)(2,1)}) %all-gather.11.cloned.1.call-update) | async-done | bytes 1572880 | tf_op jit(solution)/shard_map/all_gather | solution.py:52
  77.8 2.6 fusion.42
  80.4 96.9 %all-reduce.3.cloned.1.call-done = bf16[2,512,512]{1,2,0:T(8,128)(2,1)} async-done(((bf16[2,512,512]{1,2,0:T(8,128)(2,1)}), bf16[2,512,512]{1,2,0:T(8,128)(2,1)}) %all-reduce.3.cloned.1.call-update) | async-done | bytes 1048592 | tf_op jit(solution)/shard_map/psum | solution.py:9
  177.3 1.8 fusion.22
  179.2 1.5 fusion.24
  184.0 1.8 fusion.27
  185.8 1.8 subtract_bitcast_fusion.1
  187.6 3.1 copy.8
  190.6 3.0 copy.10
  193.7 3.6 add_bitcast_fusion.1
  197.2 3.1 copy.9
  200.3 3.0 copy.11
  203.3 2.2 fusion
  206.9 43.8 %all-gather.13.cloned.1.call-done = bf16[2,1,1024,512]{2,3,0,1:T(8,128)(2,1)} async-done(((bf16[2,1,128,512]{2,3,0,1:T(8,128)(2,1)}), bf16[2,1,1024,512]{2,3,0,1:T(8,128)(2,1)}) %all-gather.13.cloned.1.call-update) | async-done | bytes 2097168 | tf_op jit(solution)/shard_map/all_gather | solution.py:41
  250.7 2.3 slice_select_fusion
  253.1 18.1 %all-gather.15.cloned.1.call-done = bf16[1,2,6,128,512]{4,3,2,1,0:T(8,128)(2,1)} async-done(((bf16[1,2,3,128,512]{4,3,2,1,0:T(8,128)(2,1)}), bf16[1,2,6,128,512]{4,3,2,1,0:T(8,128)(2,1)}) %all-gather.15.cloned.1.call-update) | async-done | bytes 1572880 | tf_op jit(solution)/shard_map/all_gather | solution.py:52
  271.2 2.7 fusion.40
  273.8 96.7 %all-reduce.5.cloned.1.call-done = bf16[2,512,512]{1,2,0:T(8,128)(2,1)} async-done(((bf16[2,512,512]{1,2,0:T(8,128)(2,1)}), bf16[2,512,512]{1,2,0:T(8,128)(2,1)}) %all-reduce.5.cloned.1.call-update) | async-done | bytes 1048592 | tf_op jit(solution)/shard_map/psum | solution.py:9
  370.6 1.8 fusion.18
  377.3 1.8 fusion.29
  379.1 1.8 subtract_bitcast_fusion
  380.9 3.0 copy.13
  383.9 3.1 copy.15
  387.0 3.6 add_bitcast_fusion
  390.6 3.0 copy.14
  393.6 3.0 copy.16
  396.7 5.2 %fusion.1 = f32[2,6,128,512]{2,3,0,1:T(8,128)} fusion(f32[1,6,128,512]{2,3,0,1:T(8,128)} %copy.16, f32[1,6,128,512]{2,3,0,1:T(8,128)} %copy.15, pred[6,128]{1,0:T(8,128)(4,1)S(1)} %get-tuple-element.23, f32[2,6,128,512]{2,3,0,1:T(8,128)S(1)} %copy.12, f32[1,6,128,512]{2,3,0,1:T(8,128)} %copy.11, f32[1,6,128,512]{2,3,0,1:T(8,128)} %copy.10, ...), kind=kLoop, calls=%fused_computation.3 | loop fusion | flops 4718592 | bytes 12584448 | tf_op jit(solution)/shard_map/sub | solution.py:59
  404.0 3.5 copy.17
  (63 shorter events, 12.6 us)
Async XLA Ops:
  6.5 50.6 %all-gather.9.cloned.1.call-start = ((), (), s32[]{:S(2)}) async-start(), calls=%async_computation.2 | async-start | bytes 2359296 | tf_op jit(solution)/shard_map/all_gather | solution.py:41
  9.7 68.1 %all-gather.11.cloned.1.call-start = ((), (), s32[]{:S(2)}) async-start(), calls=%async_computation.3 | async-start | bytes 2359296 | tf_op jit(solution)/shard_map/all_gather | solution.py:52
  12.4 164.9 %all-reduce.3.cloned.1.call-start = ((), (), s32[]{:S(2)}) async-start(), calls=%async_computation | async-start | bytes 2097152 | tf_op jit(solution)/shard_map/psum | solution.py:9
  59.5 191.2 %all-gather.13.cloned.1.call-start = ((), (), s32[]{:S(2)}) async-start(), calls=%async_computation.4 | async-start | bytes 2359296 | tf_op jit(solution)/shard_map/all_gather | solution.py:41
  177.3 1.9 copy-start.10
  177.3 3.4 copy-start.17
  181.2 1.0 copy-start
  181.7 2.3 copy-start.2
  181.7 1.7 copy-start.12
  182.2 3.6 copy-start.8
  184.0 1.8 copy-start.14
  206.3 64.9 %all-gather.15.cloned.1.call-start = ((), (), s32[]{:S(2)}) async-start(), calls=%async_computation.5 | async-start | bytes 2359296 | tf_op jit(solution)/shard_map/all_gather | solution.py:52
  206.9 163.7 %all-reduce.5.cloned.1.call-start = ((), (), s32[]{:S(2)}) async-start(), calls=%async_computation.1 | async-start | bytes 2097152 | tf_op jit(solution)/shard_map/psum | solution.py:9
  370.6 1.9 copy-start.11
  370.6 3.4 copy-start.16
  374.5 1.0 copy-start.4
  374.9 2.3 copy-start.6
  374.9 1.7 copy-start.13
  375.4 3.6 copy-start.9
  377.3 1.8 copy-start.15
  396.7 6.3 %copy-start.1 = (f32[1,512,512]{1,2,0:T(8,128)S(1)}, f32[1,512,512]{1,2,0:T(8,128)}, u32[]{:S(2)}) copy-start(f32[1,512,512]{1,2,0:T(8,128)} %copy-done) | copy-start | bytes 3145732
  396.7 6.3 %copy-start.3 = (f32[1,512,512]{1,2,0:T(8,128)S(1)}, f32[1,512,512]{1,2,0:T(8,128)}, u32[]{:S(2)}) copy-start(f32[1,512,512]{1,2,0:T(8,128)} %copy-done.2) | copy-start | bytes 3145732
  396.7 6.3 %copy-start.5 = (f32[1,512,512]{1,2,0:T(8,128)S(1)}, f32[1,512,512]{1,2,0:T(8,128)}, u32[]{:S(2)}) copy-start(f32[1,512,512]{1,2,0:T(8,128)} %copy-done.4) | copy-start | bytes 3145732
  396.7 6.3 %copy-start.7 = (f32[1,512,512]{1,2,0:T(8,128)S(1)}, f32[1,512,512]{1,2,0:T(8,128)}, u32[]{:S(2)}) copy-start(f32[1,512,512]{1,2,0:T(8,128)} %copy-done.6) | copy-start | bytes 3145732
Sparse Core Ops, SparseCore 0:
  9.8 47.3 all-gather.8
  59.0 18.7 all-gather.10
  81.0 96.2 all-reduce.2
  206.4 44.2 all-gather.12
  252.4 18.7 all-gather.14
  274.3 96.2 all-reduce.4
where the time goes:
time: 415 us; the launch traced here: 414 us
  waiting for transfers between devices  319 us (77%)
  local copies, waits for them, and re-layouts  44 us (11%)
  matrix products  24 us (6%)
  between operations  13.7 us (3%)
  other arithmetic  13.3 us (3%)
    psum x2, waiting for transfers between devices, from_root(): return lax.psum(block, axis)  194 us
    all_gather x2, waiting for transfers between devices, per_device(): gathered = lax.all_gather(own_rows, 'col', axis=1, tiled=True)  88.5 us
    all_gather x2, waiting for transfers between devices, per_device(): panel_part = lax.all_gather(panels[step_index], 'depth', axis=1, tiled=True)  36.3 us
    another operation x4, local copies, waits for them, and re-layouts, complex_dot(): return jnp.stack([real_part, imag_part])  12.2 us
  transfers between devices with their start and end apart: 6, of which 6 were waited for; matrix products, arithmetic and copies ran while one was open for 3% of the time, Pallas kernels for 0%

commit v1 on v0

v1 whole, which is shorter than its diff:
```python
import jax
import jax.numpy as jnp
from jax import lax
from jax.experimental import pallas as pl
from jax.experimental.pallas import tpu as pltpu
from jax.sharding import PartitionSpec as P

BF = jnp.bfloat16
F32 = jnp.float32


def dot(left, right):
    return jnp.dot(left, right, preferred_element_type=F32)


def kernel(where_ref, recv_ref, other_ref, inv_ref, own_ref, swap_ref, rhs_ref, out_ref, diag, work, sol, full):
    depth = where_ref[0]
    position = where_ref[1]
    step = pl.program_id(0)
    lanes = pl.ds(pl.multiple_of(step * 128, 128), 128)

    @pl.when(step == 0)
    def _():
        for ref, which in ((recv_ref, depth), (other_ref, 1 - depth)):
            base = 128 if ref is recv_ref else 0
            for piece in range(4):
                h, w = piece // 2, piece % 2
                for r in range(16):
                    diag[which, piece * 128 + 16 * (r // 2) : piece * 128 + 16 * (r // 2) + 16, 256 * (r % 2) : 256 * (r % 2) + 256] = ref[
                        r, base + 16 * h : base + 16 * h + 16, 256 * w : 256 * w + 256
                    ]

    def put(ref, at, real, imag):
        rows = real.shape[0]
        ref[at : at + rows, 0:128] = real
        ref[at : at + rows, 128:256] = imag
        ref[512 + at : 512 + at + rows, 0:128] = -imag
        ref[512 + at : 512 + at + rows, 128:256] = real

    def block(s, part):
        return jnp.concatenate(
            [recv_ref[8 * part + rr, (4 * s + zz) * 16 : (4 * s + zz) * 16 + 16, lanes] for zz in range(4) for rr in range(8)], axis=0
        )

    def solve(s):
        top = dot(inv_ref[s, 0, :256, :256], work[0:256]) + dot(inv_ref[s, 1, :256, :256], work[512:768])
        low = dot(inv_ref[s, 0, 256:, :], work[0:512]) + dot(inv_ref[s, 1, 256:, :], work[512:1024])
        for at, value in ((0, top), (256, low)):
            full[s, at : at + 256] = value
            half = value.astype(BF)
            put(sol.at[s], at, half[:, :128], half[:, 128:])

    put(work, 0, block(0, 0), block(0, 1))
    solve(0)
    taken = dot(diag[0], sol[0, 0:512]) + dot(diag[1], sol[0, 512:1024])
    put(
        work,
        0,
        (block(1, 0).astype(F32) - taken[:, :128]).astype(BF),
        (block(1, 1).astype(F32) - taken[:, 128:]).astype(BF),
    )
    solve(1)
    for ref, first in ((own_ref, depth * 3), (swap_ref, 3 - depth * 3)):
        total = None
        for s in range(2):
            for part in range(2):
                term = dot(ref[s, part].reshape(384, 512), sol[s, 512 * part : 512 * part + 512])
                total = term if total is None else total + term
        for part in range(2):
            old = rhs_ref[part, pl.ds(first, 3)]
            out_ref[part, pl.ds(first, 3)] = old - total[:, 128 * part : 128 * part + 128].reshape(3, 128, 128)

    @pl.when(position < 8)
    def _():
        rows = pl.ds(pl.multiple_of((position % 4) * 128, 128), 128)
        for part in range(2):
            out_ref[part, 0] = full[position // 4, rows, 128 * part : 128 * part + 128]


def update(where, recv, other, inverses, own, swap, rhs):
    whole = pl.BlockSpec(memory_space=pltpu.VMEM)
    tile = pl.BlockSpec((2, 6, 128, 128), lambda i: (0, 0, 0, i))
    return pl.pallas_call(
        kernel,
        grid=(4,),
        in_specs=[pl.BlockSpec(memory_space=pltpu.SMEM)] + [whole] * 5 + [tile],
        out_specs=tile,
        out_shape=jax.ShapeDtypeStruct(rhs.shape, F32),
        scratch_shapes=[
            pltpu.VMEM((2, 512, 512), BF),
            pltpu.VMEM((1024, 256), BF),
            pltpu.VMEM((2, 1024, 256), BF),
            pltpu.VMEM((2, 512, 256), F32),
        ],
        compiler_params=pltpu.CompilerParams(vmem_limit_bytes=48 * 1024 * 1024),
        cost_estimate=pl.CostEstimate(flops=6_400_000_000, bytes_accessed=12_000_000, transcendentals=0),
    )(where, recv, other, inverses, own, swap, rhs)


def per_device(rhs, panels, inverses):
    depth = lax.axis_index("depth")
    position = lax.axis_index(("row", "col"))
    where = jnp.stack([depth, position]).astype(jnp.int32)
    first = panels[0, :, 0]
    passed = lax.ppermute(first[1], "depth", [(0, 1), (1, 0)])
    mine = jnp.where(depth == 0, first[0], passed)
    swap = lax.ppermute(panels, "depth", [(0, 1), (1, 0)])
    rows = rhs[:, 0].astype(BF).reshape(16, 16, 512)
    mine = mine.reshape(8, 16, 2, 256).transpose(0, 2, 1, 3).reshape(16, 16, 256)
    dealt = lax.all_to_all(jnp.concatenate([rows, mine], axis=2), "row", 0, 0, tiled=True)[0]
    line = lax.all_to_all(jnp.broadcast_to(dealt, (8, 16, 768)), "col", 0, 0, tiled=True)
    tail = line[4:, :, 512:].reshape(2, 2, 16, 256).transpose(0, 2, 1, 3).reshape(32, 512)
    share = jnp.concatenate([line[:, :, :512].reshape(128, 512), tail], axis=0)
    recv = lax.all_to_all(jnp.broadcast_to(share, (16, 160, 512)), "row", 0, 0, tiled=True)
    other = lax.ppermute(recv[:, 128:], "depth", [(0, 1), (1, 0)])
    return update(where, recv, other, inverses, panels.reshape(2, 2, 3, 128, 512), swap, rhs)


def solution(mesh):
    return jax.shard_map(
        per_device,
        mesh=mesh,
        in_specs=(
            P(None, None, ("row", "col"), "depth"),
            P(None, None, "depth", ("row", "col"), None),
            P(),
        ),
        out_specs=P(None, None, ("row", "col"), "depth"),
        check_vma=False,
    )
```

time: 415 us -> 98.9 us (0.24)
  waiting for transfers between devices: 319 us -> 29.4 us
  local copies, waits for them, and re-layouts: 44 us -> 7.33 us
  blocking collectives: 0 us -> 30.8 us
  matrix products: 24 us -> 0 us
  starting transfers between devices: 0.21 us -> 16.9 us
  between operations: 13.7 us -> 0.1 us
  Pallas kernels: 0 us -> 13 us
  other arithmetic: 13.3 us -> 1.04 us
    psum x2 -> x0, waiting for transfers between devices: 194 us -> none  [from_root(): return lax.psum(block, axis)]
    all_gather x4 -> x0, waiting for transfers between devices: 125 us -> none  [the longest x2 88.5 us: per_device(): gathered = lax.all_gather(own_rows, 'col', axis=1, tiled=True)]
    all_to_all x0 -> x2, blocking collectives: none -> 30.8 us  [the longest x1 16.6 us: per_device(): lax.all_to_all(jnp.broadcast_to(dealt, (8, 16, 768)), 'col', 0, 0, tiled=...]
    all_to_all x0 -> x1, waiting for transfers between devices: none -> 27.6 us  [per_device(): lax.all_to_all(jnp.broadcast_to(share, (16, 160, 512)), 'row', 0, 0, tile...]
    dot_general x16 -> x0, matrix products: 24 us -> none  [the longest x4 8.09 us: complex_dot(): jnp.dot(left_imag, right_real, preferred_element_type=jnp.float32)]
    pallas_call x0 -> x1, Pallas kernels: none -> 13 us  [update(): pl.pallas_call(kernel, grid=(4,), in_specs=[pl.BlockSpec(memory_space=plt...]
    ppermute x0 -> x3, starting transfers between devices: none -> 12.3 us  [the longest x1 6.01 us: per_device(): other = lax.ppermute(recv[:, 128:], 'depth', [(0, 1), (1, 0)])]
    another operation x4 -> x0, local copies, waits for them, and re-layouts: 12.2 us -> none  [complex_dot(): return jnp.stack([real_part, imag_part])]
  transfers between devices with their start and end apart: 6 -> 4, of which waited for: 6 -> 2; matrix products, arithmetic and copies ran while one was open for 3% -> 3% of each run, Pallas kernels for 0% -> 0%
where the time goes in v1:
time: 98.9 us; the launch traced here: 98.5 us
  blocking collectives  30.8 us (31%)
  waiting for transfers between devices  29.4 us (30%)
  starting transfers between devices  16.9 us (17%)
  Pallas kernels  13 us (13%)
  local copies, waits for them, and re-layouts  7.33 us (7%)
  other arithmetic  1.04 us (1%)
    all_to_all x1, waiting for transfers between devices, per_device(): lax.all_to_all(jnp.broadcast_to(share, (16, 160, 512)), 'row', 0, 0, tile...  27.6 us
    all_to_all x1, blocking collectives, per_device(): lax.all_to_all(jnp.broadcast_to(dealt, (8, 16, 768)), 'col', 0, 0, tiled=...  16.6 us
    all_to_all x1, blocking collectives, per_device(): lax.all_to_all(jnp.concatenate([rows, mine], axis=2), 'row', 0, 0, tiled=...  14.1 us
    pallas_call x1, Pallas kernels, update(): pl.pallas_call(kernel, grid=(4,), in_specs=[pl.BlockSpec(memory_space=plt...  13 us
    ppermute x1, starting transfers between devices, per_device(): other = lax.ppermute(recv[:, 128:], 'depth', [(0, 1), (1, 0)])  6.01 us
    all_to_all x1, starting transfers between devices, per_device(): lax.all_to_all(jnp.broadcast_to(share, (16, 160, 512)), 'row', 0, 0, tile...  4.59 us
    ppermute x1, starting transfers between devices, per_device(): passed = lax.ppermute(first[1], 'depth', [(0, 1), (1, 0)])  3.33 us
    ppermute x1, starting transfers between devices, per_device(): swap = lax.ppermute(panels, 'depth', [(0, 1), (1, 0)])  2.97 us
  transfers between devices with their start and end apart: 4, of which 2 were waited for; matrix products, arithmetic and copies ran while one was open for 3% of the time, Pallas kernels for 0%

profile of v1, /device:TPU:1, one launch (start us, length us, event | category | flops | bytes accessed | tf_op | source)
XLA Modules:
  0.0 98.5 jit_solution(7833996939977956835)
XLA Ops:
  0.0 0.9 slice_bitcast_fusion
  0.9 3.3 %collective-permute-start = (bf16[128,512]{1,0:T(8,128)(2,1)S(1)}, bf16[128,512]{1,0:T(8,128)(2,1)S(1)}, u32[]{:S(2)}, u32[]{:S(2)}) collective-permute-start(bf16[128,512]{1,0:T(8,128)(2,1)S(1)} %slice_bitcast_fusion), channel_id=1, source_target_pairs={{0,128},{128,0},{1,129},{129,1},{2,130},{130,2},{3,131},{131,3},{4... | collective-permute-start | bytes 393224 | tf_op jit(solution)/shard_map/ppermute | solution.py:105
  4.2 1.1 %slice.43 = bf16[2,1,128,512]{3,2,1,0:T(8,128)(2,1)S(1)} slice(f32[2,6,128,512]{3,2,1,0:T(8,128)} %rhs_ref.1), slice={[0:2], [0:1], [0:128], [0:512]} | slice | bytes 524288 | tf_op jit(solution)/shard_map/slice | solution.py:108
  5.3 0.0 collective-permute-done
  5.3 0.9 bitcast_select_fusion
  6.4 14.1 %all_to_all.15 = bf16[16,16,768]{2,1,0:T(8,128)(2,1)S(1)} all-to-all(bf16[16,16,768]{2,1,0:T(8,128)(2,1)S(1)} %pad_maximum_fusion), channel_id=1, replica_groups=mesh['depth'=2,'row'=16,'col'=8] {'row'}, dimensions={0} | all-to-all | bytes 786432 | tf_op jit(solution)/shard_map/all_to_all | solution.py:110
  20.5 16.6 %all_to_all.16 = bf16[8,16,768]{2,1,0:T(8,128)(2,1)S(1)} all-to-all(bf16[8,16,768]{2,1,0:T(8,128)(2,1)S(1)} %broadcast_in_dim.6), channel_id=1, replica_groups=mesh['depth'=2,'row'=16,'col'=8] {'col'}, dimensions={0} | all-to-all | bytes 393216 | tf_op jit(solution)/shard_map/all_to_all | solution.py:111
  37.2 1.7 %broadcast_in_dim.7 = bf16[16,160,512]{2,1,0:T(8,128)(2,1)} broadcast(bf16[160,512]{1,0:T(8,128)(2,1)S(1)} %pad_maximum_fusion.1), dimensions={1,2} | broadcast | bytes 2785280 | tf_op jit(solution)/shard_map/broadcast_in_dim | solution.py:114
  39.0 0.0 copy-start
  39.0 4.6 %all-to-all-start.2 = ((bf16[16,160,512]{2,1,0:T(8,128)(2,1)}), bf16[16,160,512]{2,1,0:T(8,128)(2,1)}, u32[]{:S(2)}, u32[]{:S(2)}) async-start(bf16[16,160,512]{2,1,0:T(8,128)(2,1)} %broadcast_in_dim.7), calls=%async_computation.2 | async-start | bytes 5242880 | tf_op jit(solution)/shard_map/all_to_all | solution.py:114
  43.6 0.0 copy-done
  43.6 3.0 %collective-permute-start.2 = (bf16[2,2,3,128,512]{4,3,2,1,0:T(8,128)(2,1)S(1)}, bf16[2,2,3,128,512]{4,3,2,1,0:T(8,128)(2,1)S(1)}, u32[]{:S(2)}, u32[]{:S(2)}) collective-permute-start(bf16[2,2,3,128,512]{4,3,2,1,0:T(8,128)(2,1)S(1)} %copy-done), channel_id=1, source_target_pairs={{0,128},{128,0},{1,129},{129,1},{2,130},{130,2},{3,131},{131,3},{4... | collective-permute-start | bytes 4718600 | tf_op jit(solution)/shard_map/ppermute | solution.py:107
  46.6 27.6 %all-to-all-done.2.recv_ref = bf16[16,160,512]{2,1,0:T(8,128)(2,1)} async-done(((bf16[16,160,512]{2,1,0:T(8,128)(2,1)}), bf16[16,160,512]{2,1,0:T(8,128)(2,1)}, u32[]{:S(2)}, u32[]{:S(2)}) %all-to-all-start.2) | async-done | bytes 2621472 | tf_op jit(solution)/shard_map/all_to_all | solution.py:114
  74.1 1.9 %slice.38 = bf16[16,32,512]{2,1,0:T(8,128)(2,1)} slice(bf16[16,160,512]{2,1,0:T(8,128)(2,1)} %all-to-all-done.2.recv_ref), slice={[0:16], [128:160], [0:512]} | slice | bytes 1048576 | tf_op jit(solution)/shard_map/slice | solution.py:115
  76.0 6.0 %collective-permute-start.1 = (bf16[16,32,512]{2,1,0:T(8,128)(2,1)}, bf16[16,32,512]{2,1,0:T(8,128)(2,1)}, u32[]{:S(2)}, u32[]{:S(2)}) collective-permute-start(bf16[16,32,512]{2,1,0:T(8,128)(2,1)} %slice.38), channel_id=1, source_target_pairs={{0,128},{128,0},{1,129},{129,1},{2,130},{130,2},{3,131},{131,3},{4... | collective-permute-start | bytes 1572872 | tf_op jit(solution)/shard_map/ppermute | solution.py:115
  82.0 0.1 pad_add_fusion.where_ref
  82.1 0.0 collective-permute-done.2.swap_ref
  82.1 1.8 %collective-permute-done.1.other_ref = bf16[16,32,512]{2,1,0:T(8,128)(2,1)} collective-permute-done((bf16[16,32,512]{2,1,0:T(8,128)(2,1)}, bf16[16,32,512]{2,1,0:T(8,128)(2,1)}, u32[]{:S(2)}, u32[]{:S(2)}) %collective-permute-start.1) | collective-permute-done | bytes 524320 | tf_op jit(solution)/shard_map/ppermute | solution.py:115
  83.9 0.0 copy-start.1
  83.9 1.6 %copy-done.1 = bf16[2,2,512,512]{3,2,1,0:T(8,128)(2,1)S(1)} copy-done((bf16[2,2,512,512]{3,2,1,0:T(8,128)(2,1)S(1)}, bf16[2,2,512,512]{3,2,1,0:T(8,128)(2,1)}, u32[]{:S(2)}) %copy-start.1) | copy-done | bytes 2097176
  85.5 13.0 %shard_map.37 = f32[2,6,128,512]{3,2,1,0:T(8,128)} custom-call(s32[2]{0:T(128)S(1)} %pad_add_fusion.where_ref, bf16[16,160,512]{2,1,0:T(8,128)(2,1)} %all-to-all-done.2.recv_ref, bf16[16,32,512]{2,1,0:T(8,128)(2,1)} %collective-permute-done.1.other_ref, bf16[2,2,512,512]{3,2,1,0:T(8,128)(2,1)S(1)} %copy-done.1, bf16[2,2,3,128,512]{4,3,2,1,0:T(8,128)(2,1)S(1)} %copy-done, ...), custom_call_target="tpu_custom_call" | custom-call | flops 6400000000 | bytes 12000000 | tf_op jit(solution)/shard_map/pallas_call | solution.py:83
  (10 shorter events, 0.2 us)
Async XLA Ops:
  0.9 4.4 %collective-permute-start = (bf16[128,512]{1,0:T(8,128)(2,1)S(1)}, bf16[128,512]{1,0:T(8,128)(2,1)S(1)}, u32[]{:S(2)}, u32[]{:S(2)}) collective-permute-start(bf16[128,512]{1,0:T(8,128)(2,1)S(1)} %slice_bitcast_fusion), channel_id=1, source_target_pairs={{0,128},{128,0},{1,129},{129,1},{2,130},{130,2},{3,131},{131,3},{4... | collective-permute-start | bytes 393224 | tf_op jit(solution)/shard_map/ppermute | solution.py:105
  39.0 4.6 %copy-start = (bf16[2,2,3,128,512]{4,3,2,1,0:T(8,128)(2,1)S(1)}, bf16[2,2,3,128,512]{4,3,2,1,0:T(8,128)(2,1)}, u32[]{:S(2)}) copy-start(bf16[2,2,3,128,512]{4,3,2,1,0:T(8,128)(2,1)} %own_ref.1) | copy-start | bytes 4718596
  39.0 35.2 %all-to-all-start.2 = ((bf16[16,160,512]{2,1,0:T(8,128)(2,1)}), bf16[16,160,512]{2,1,0:T(8,128)(2,1)}, u32[]{:S(2)}, u32[]{:S(2)}) async-start(bf16[16,160,512]{2,1,0:T(8,128)(2,1)} %broadcast_in_dim.7), calls=%async_computation.2 | async-start | bytes 5242880 | tf_op jit(solution)/shard_map/all_to_all | solution.py:114
  43.6 38.5 %collective-permute-start.2 = (bf16[2,2,3,128,512]{4,3,2,1,0:T(8,128)(2,1)S(1)}, bf16[2,2,3,128,512]{4,3,2,1,0:T(8,128)(2,1)S(1)}, u32[]{:S(2)}, u32[]{:S(2)}) collective-permute-start(bf16[2,2,3,128,512]{4,3,2,1,0:T(8,128)(2,1)S(1)} %copy-done), channel_id=1, source_target_pairs={{0,128},{128,0},{1,129},{129,1},{2,130},{130,2},{3,131},{131,3},{4... | collective-permute-start | bytes 4718600 | tf_op jit(solution)/shard_map/ppermute | solution.py:107
  76.0 7.9 %collective-permute-start.1 = (bf16[16,32,512]{2,1,0:T(8,128)(2,1)}, bf16[16,32,512]{2,1,0:T(8,128)(2,1)}, u32[]{:S(2)}, u32[]{:S(2)}) collective-permute-start(bf16[16,32,512]{2,1,0:T(8,128)(2,1)} %slice.38), channel_id=1, source_target_pairs={{0,128},{128,0},{1,129},{129,1},{2,130},{130,2},{3,131},{131,3},{4... | collective-permute-start | bytes 1572872 | tf_op jit(solution)/shard_map/ppermute | solution.py:115
  83.9 1.6 %copy-start.1 = (bf16[2,2,512,512]{3,2,1,0:T(8,128)(2,1)S(1)}, bf16[2,2,512,512]{3,2,1,0:T(8,128)(2,1)}, u32[]{:S(2)}) copy-start(bf16[2,2,512,512]{3,2,1,0:T(8,128)(2,1)} %inv_ref.1) | copy-start | bytes 6291460

commit v2 on v0

v2 whole, which is shorter than its diff:
```python
import jax
import jax.numpy as jnp
from jax import lax
from jax.experimental import pallas as pl
from jax.experimental.pallas import tpu as pltpu
from jax.sharding import PartitionSpec as P

BF = jnp.bfloat16
F32 = jnp.float32
SWAP = [(0, 1), (1, 0)]
AXES = ("depth", "row", "col")
SIDE = 4
SHIFTS = (0, 1, 3, 2)
TILES = 4


def place(depth, x, y, z):
    return (depth * 16 + (x % SIDE) * SIDE + y % SIDE) * 8 + z


def plane_groups():
    return [
        [place(d, c // 4, c % 4, z) if d == 0 else place(d, c % 4, c // 4, z) for c in range(16)] for d in range(2) for z in range(8)
    ]


def slow_groups():
    return [
        [place(d, m, o, z) if d == 0 else place(d, o, m, z) for m in range(4)] for d in range(2) for z in range(8) for o in range(4)
    ]


def fast_shift(by):
    return [
        (place(d, x, y, z), place(d, x, y + by, z) if d == 0 else place(d, x + by, y, z))
        for d in range(2)
        for x in range(4)
        for y in range(4)
        for z in range(8)
    ]


def dot(left, right):
    return jnp.dot(left, right, preferred_element_type=F32)


def fill(copies, sems, start=0):
    copies = [pltpu.make_async_copy(source, target, sems.at[start + i]) for i, (source, target) in enumerate(copies)]
    for copy in copies:
        copy.start()
    return copies


def matrices(s, depth, inv_ref, own_ref, swap_ref, inv, panel):
    copies = [(inv_ref.at[s, part, :, 256 * k : 256 * k + 256], inv.at[:, 512 * k + 256 * part : 512 * k + 256 * part + 256]) for k in range(2) for part in range(2)]
    return copies + [
        (ref.at[s, part], panel.at[pl.ds(first, 3), :, 512 * part : 512 * part + 512])
        for part in range(2)
        for ref, first in ((own_ref, depth * 3), (swap_ref, 3 - depth * 3))
    ]


def places(where_ref):
    depth, position = where_ref[0], where_ref[1]
    place_x, place_y = position >> 5, (position >> 3) & 3
    group = jnp.where(depth == 0, place_y, place_x)
    return depth, position, group, place_x + place_y - group


def put(ref, at, back, value):
    rows = value.shape[0]
    for j in range(TILES):
        real, imag = value[:, 256 * j : 256 * j + 128], value[:, 256 * j + 128 : 256 * j + 256]
        ref[at : at + rows, 256 * j : 256 * j + 128] = real
        ref[at : at + rows, 256 * j + 128 : 256 * j + 256] = imag
        ref[back : back + rows, 256 * j : 256 * j + 128] = -imag
        ref[back : back + rows, 256 * j + 128 : 256 * j + 256] = real


def block(held, s, k):
    return jnp.concatenate(
        [
            jnp.concatenate(
                [ref[m, ((4 * s + zz) * 2 + part) * 32 : ((4 * s + zz) * 2 + part) * 32 + 32, :] for zz in (2 * k, 2 * k + 1) for m in range(4)], axis=0
            )
            for ref in held
            for part in range(2)
        ],
        axis=1,
    )


def solve(inv, work, sol, piece, rows):
    value = dot(inv[:, 0:512], work[0:512])
    low = value[256:] + dot(inv[256:, 512:1024], work[512:1024])
    for at, part in ((0, value[:256]), (256, low)):
        put(sol, at, 512 + at, part.astype(BF))

        @pl.when((rows >> 8) == (at >> 8))
        def _():
            piece[...] = jnp.where((rows & 128) == 0, part[:128], part[128:])


def fill_diag(diag, halves, first):
    for half, shift in zip(halves, SHIFTS):
        at = pl.multiple_of(((first + 4 - shift) & 3) * 128, 128)
        for m in range(4):
            for zz in range(4):
                diag[zz * 128 + m * 32 : zz * 128 + m * 32 + 32, pl.ds(at, 128)] = half[m, zz * 32 : zz * 32 + 32, :]


def first_kernel(where_ref, h0, h1, h2, h3, inv_ref, own_ref, swap_ref, rhs_ref, sol, state, left, inv1, panel1, inv0, panel0, diag, work, piece, sems):
    depth, position, group, _ = places(where_ref)
    held = (h0, h1, h2, h3)
    loads = fill(matrices(0, depth, inv_ref, own_ref, swap_ref, inv0, panel0), sems)
    loads_rhs = fill(
        [(rhs_ref.at[:, :, :, pl.ds(pl.multiple_of(((group + 4 - shift) & 3) * 128, 128), 128)], state.at[j]) for j, shift in enumerate(SHIFTS)], sems, 8
    )
    loads_next = fill(matrices(1, depth, inv_ref, own_ref, swap_ref, inv1, panel1), sems, 12)
    for k in range(2):
        put(work, 512 * k, 512 * k + 256, block(held, 0, k))
    fill_diag(diag, [ref.at[:, 512:640] for ref in held], group)
    for load in loads[:4]:
        load.wait()
    solve(inv0, work, sol, piece, (position & 3) * 128)
    ours = pl.ds(pl.multiple_of(depth * 512, 512), 512)
    for k in range(2):
        left[256 * k : 256 * k + 256] = block(held, 1, k).astype(F32) - dot(diag[256 * k : 256 * k + 256], sol[ours])
    for load in loads[4:] + loads_rhs:
        load.wait()
    for c in range(0, 6, 3):
        total = dot(panel0[c : c + 3].reshape(384, 1024), sol[...])
        for j in range(TILES):
            for part in range(2):
                at = 256 * j + 128 * part
                state[j, part, c : c + 3] = state[j, part, c : c + 3] - total[:, at : at + 128].reshape(3, 128, 128)

    @pl.when(position < 4)
    def _():
        for j in range(TILES):
            for part in range(2):
                at = 256 * j + 128 * part
                state[j, part, 0] = piece[:, at : at + 128]

    for load in loads_next:
        load.wait()


def second_kernel(where_ref, sol0, state, left, inv, panel, other_ref, out_ref, half, diag, work, sol, piece, new, sems, out_sems):
    depth, position, group, other_group = places(where_ref)
    (load,) = fill([(other_ref, half)], sems)
    load.wait()
    fill_diag(diag, [half.at[j] for j in range(TILES)], other_group)
    theirs = pl.ds(pl.multiple_of((1 - depth) * 512, 512), 512)
    for k in range(2):
        put(work, 512 * k, 512 * k + 256, (left[256 * k : 256 * k + 256] - dot(diag[256 * k : 256 * k + 256], sol0[theirs])).astype(BF))
    solve(inv, work, sol, piece, (position & 3) * 128)
    stores = []
    for c in range(0, 6, 2):
        total = dot(panel[c : c + 2].reshape(256, 1024), sol[...])
        for j in range(TILES):
            for part in range(2):
                at = 256 * j + 128 * part
                new[j, part, c : c + 2] = state[j, part, c : c + 2] - total[:, at : at + 128].reshape(2, 128, 128)
        if c == 0:
            @pl.when(position < 8)
            def _():
                for j in range(TILES):
                    for part in range(2):
                        at = 256 * j + 128 * part
                        new[j, part, 0] = jnp.where(position < 4, state[j, part, 0], piece[:, at : at + 128])

        stores += fill(
            [
                (new.at[j, :, c : c + 2], out_ref.at[:, c : c + 2, :, pl.ds(pl.multiple_of(((group + 4 - shift) & 3) * 128, 128), 128)])
                for j, shift in enumerate(SHIFTS)
            ],
            out_sems,
            2 * c,
        )
    for store in stores:
        store.wait()


def update(where, inverses, own, swap, rhs, held, other):
    smem = pl.BlockSpec(memory_space=pltpu.SMEM)
    hbm = pl.BlockSpec(memory_space=pl.ANY)
    vmem = pl.BlockSpec(memory_space=pltpu.VMEM)

    def call(body, cost, out_shape, scratch, *operands):
        return pl.pallas_call(
            body,
            in_specs=[smem] + [vmem if isinstance(value, list) else hbm for value in operands],
            out_specs=[vmem if isinstance(shape, pl.MemoryRef) else hbm for shape in out_shape],
            out_shape=out_shape,
            scratch_shapes=scratch,
            compiler_params=pltpu.CompilerParams(vmem_limit_bytes=14 * 1024 * 1024),
            cost_estimate=pl.CostEstimate(flops=cost, bytes_accessed=cost // 400, transcendentals=0),
        )(where, *[pltpu.with_memory_space_constraint(value[0], pltpu.VMEM) if isinstance(value, list) else value for value in operands])

    fixed = [pltpu.with_memory_space_constraint(value, pltpu.HBM) for value in (inverses, own, swap, rhs)]
    sol, state, left, inv, panel = call(
        first_kernel,
        3_000_000_000,
        [
            pltpu.VMEM((1024, 1024), BF),
            pltpu.VMEM((TILES, 2, 6, 128, 128), F32),
            pltpu.VMEM((512, 1024), F32),
            pltpu.VMEM((512, 1024), BF),
            pltpu.VMEM((6, 128, 1024), BF),
        ],
        [
            pltpu.VMEM((512, 1024), BF),
            pltpu.VMEM((6, 128, 1024), BF),
            pltpu.VMEM((512, 512), BF),
            pltpu.VMEM((1024, 1024), BF),
            pltpu.VMEM((128, 1024), F32),
            pltpu.SemaphoreType.DMA((20,)),
        ],
        *[[part] for part in held],
        *fixed,
    )
    (out,) = call(
        second_kernel,
        3_000_000_000,
        [jax.ShapeDtypeStruct(rhs.shape, F32)],
        [
            pltpu.VMEM((TILES, 4, 128, 128), BF),
            pltpu.VMEM((512, 512), BF),
            pltpu.VMEM((1024, 1024), BF),
            pltpu.VMEM((1024, 1024), BF),
            pltpu.VMEM((128, 1024), F32),
            pltpu.VMEM((TILES, 2, 6, 128, 128), F32),
            pltpu.SemaphoreType.DMA((1,)),
            pltpu.SemaphoreType.DMA((12,)),
        ],
        *[[value] for value in (sol, state, left, inv, panel)],
        other,
    )
    return out


def all_to_all(value, groups):
    return lax.all_to_all(value, AXES, 0, 0, axis_index_groups=groups, tiled=True)


def per_device(rhs, panels, inverses):
    depth = lax.axis_index("depth")
    position = lax.axis_index(("row", "col"))
    where = jnp.stack([depth, position]).astype(jnp.int32)
    first = panels[0, :, 0]
    passed = lax.ppermute(first[1], "depth", SWAP)
    mine = jnp.where(depth == 0, first[0], passed)
    swap = lax.ppermute(panels, "depth", SWAP)
    rows = rhs[:, 0].astype(BF).reshape(2, 4, 32, 4, 128).transpose(1, 3, 0, 2, 4).reshape(16, 64, 128)
    mine = mine.reshape(4, 32, 4, 128).transpose(0, 2, 1, 3).reshape(16, 32, 128)
    dealt = all_to_all(jnp.concatenate([rows, mine], axis=1), plane_groups())[0]
    line = lax.all_to_all(jnp.broadcast_to(dealt, (8, 96, 128)), "col", 0, 0, tiled=True)
    share = jnp.concatenate([line[:, :64].reshape(512, 128), line[4:, 64:].reshape(128, 128)], axis=0)
    held = all_to_all(jnp.broadcast_to(share, (4, 640, 128)), slow_groups())
    parts = [held] + [lax.ppermute(held, AXES, fast_shift(shift)) for shift in SHIFTS[1:]]
    other = lax.ppermute(jnp.stack([part[:, 512:] for part in parts]), "depth", SWAP)
    return update(where, inverses, panels, swap, rhs, parts, other)


def solution(mesh):
    return jax.shard_map(
        per_device,
        mesh=mesh,
        in_specs=(
            P(None, None, ("row", "col"), "depth"),
            P(None, None, "depth", ("row", "col"), None),
            P(),
        ),
        out_specs=P(None, None, ("row", "col"), "depth"),
        check_vma=False,
    )
```

time: 415 us -> 84 us (0.20)
  waiting for transfers between devices: 319 us -> 11.2 us
  local copies, waits for them, and re-layouts: 44 us -> 2.33 us
  blocking collectives: 0 us -> 41.1 us
  matrix products: 24 us -> 0 us
  starting transfers between devices: 0.21 us -> 15.2 us
  between operations: 13.7 us -> 0.12 us
  Pallas kernels: 0 us -> 11.7 us
  other arithmetic: 13.3 us -> 1.9 us
    psum x2 -> x0, waiting for transfers between devices: 194 us -> none  [from_root(): return lax.psum(block, axis)]
    all_gather x4 -> x0, waiting for transfers between devices: 125 us -> none  [the longest x2 88.5 us: per_device(): gathered = lax.all_gather(own_rows, 'col', axis=1, tiled=True)]
    all_to_all x0 -> x3, blocking collectives: none -> 41.1 us  [the longest x2 24.6 us: all_to_all(): lax.all_to_all(value, AXES, 0, 0, axis_index_groups=groups, tiled=True)]
    dot_general x16 -> x0, matrix products: 24 us -> none  [the longest x4 8.09 us: complex_dot(): jnp.dot(left_imag, right_real, preferred_element_type=jnp.float32)]
    ppermute x0 -> x6, starting transfers between devices: none -> 15.2 us  [the longest x1 4.91 us: per_device(): lax.ppermute(jnp.stack([part[:, 512:] for part in parts]), 'depth', SWAP)]
    another operation x4, local copies, waits for them, and re-layouts: 12.2 us -> 0.04 us  [per_device(): jnp.stack([part[:, 512:] for part in parts])]
    pallas_call x0 -> x2, Pallas kernels: none -> 11.7 us  [call(): pl.pallas_call(body, in_specs=[smem] + [vmem if isinstance(value, list) e...]
    ppermute x0 -> x6, waiting for transfers between devices: none -> 11.2 us  [the longest x3 11.2 us: per_device(): lax.ppermute(held, AXES, fast_shift(shift))]
  transfers between devices with their start and end apart: 6 -> 6, of which waited for: 6 -> 3; matrix products, arithmetic and copies ran while one was open for 3% -> 3% of each run, Pallas kernels for 0% -> 7%
where the time goes in v2:
time: 84 us; the launch traced here: 83.7 us
  blocking collectives  41.1 us (49%)
  starting transfers between devices  15.2 us (18%)
  Pallas kernels  11.7 us (14%)
  waiting for transfers between devices  11.2 us (13%)
  local copies, waits for them, and re-layouts  2.33 us (3%)
  other arithmetic  1.9 us (2%)
    all_to_all x2, blocking collectives, all_to_all(): lax.all_to_all(value, AXES, 0, 0, axis_index_groups=groups, tiled=True)  24.6 us
    all_to_all x1, blocking collectives, per_device(): lax.all_to_all(jnp.broadcast_to(dealt, (8, 96, 128)), 'col', 0, 0, tiled=...  16.5 us
    pallas_call x2, Pallas kernels, call(): pl.pallas_call(body, in_specs=[smem] + [vmem if isinstance(value, list) e...  11.7 us
    ppermute x3, waiting for transfers between devices, per_device(): lax.ppermute(held, AXES, fast_shift(shift))  11.2 us
    ppermute x1, starting transfers between devices, per_device(): lax.ppermute(jnp.stack([part[:, 512:] for part in parts]), 'depth', SWAP)  4.91 us
    ppermute x1, starting transfers between devices, per_device(): swap = lax.ppermute(panels, 'depth', SWAP)  4.77 us
    ppermute x1, starting transfers between devices, per_device(): passed = lax.ppermute(first[1], 'depth', SWAP)  3.33 us
    ppermute x3, starting transfers between devices, per_device(): lax.ppermute(held, AXES, fast_shift(shift))  2.21 us
  transfers between devices with their start and end apart: 6, of which 3 were waited for; matrix products, arithmetic and copies ran while one was open for 3% of the time, Pallas kernels for 7%

profile of v2, /device:TPU:1, one launch (start us, length us, event | category | flops | bytes accessed | tf_op | source)
XLA Modules:
  0.0 83.7 jit_solution(3093665449411119993)
XLA Ops:
  0.0 0.9 %slice_bitcast_fusion.4 = bf16[128,512]{1,0:T(8,128)(2,1)S(1)} fusion(bf16[2,2,3,128,512]{4,3,2,1,0:T(8,128)(2,1)} %own_ref.1), kind=kLoop, calls=%fused_computation.9 | loop fusion | bytes 262144 | tf_op jit(solution)/shard_map/squeeze | solution.py:252
  0.9 3.3 %collective-permute-start = (bf16[128,512]{1,0:T(8,128)(2,1)S(1)}, bf16[128,512]{1,0:T(8,128)(2,1)S(1)}, u32[]{:S(2)}, u32[]{:S(2)}) collective-permute-start(bf16[128,512]{1,0:T(8,128)(2,1)S(1)} %slice_bitcast_fusion.4), channel_id=1, source_target_pairs={{0,128},{128,0},{1,129},{129,1},{2,130},{130,2},{3,131},{131,3},{4... | collective-permute-start | bytes 393224 | tf_op jit(solution)/shard_map/ppermute | solution.py:252
  4.2 1.1 %slice.62 = bf16[2,1,128,512]{3,2,1,0:T(8,128)(2,1)S(1)} slice(f32[2,6,128,512]{3,2,1,0:T(8,128)} %rhs_ref.1), slice={[0:2], [0:1], [0:128], [0:512]} | slice | bytes 524288 | tf_op jit(solution)/shard_map/slice | solution.py:255
  5.3 0.1 convert_element_type.5
  5.5 0.0 collective-permute-done
  5.5 0.9 %bitcast_select_fusion = bf16[128,512]{1,0:T(8,128)(2,1)S(1)} fusion(bf16[128,512]{1,0:T(8,128)(2,1)S(1)} %collective-permute-done, bf16[2,2,3,128,512]{4,3,2,1,0:T(8,128)(2,1)} %own_ref.1, pred[]{:T(512)S(6)} %eq.3), kind=kLoop, calls=%fused_computation.8 | loop fusion | flops 65536 | bytes 393217 | tf_op jit(solution)/shard_map/jit(_where)/select_n | solution.py:253
  6.5 14.6 %all_to_all.15 = bf16[16,96,128]{2,1,0:T(8,128)(2,1)S(1)} all-to-all(bf16[16,96,128]{2,1,0:T(8,128)(2,1)S(1)} %pad_maximum_fusion.1), channel_id=1, replica_groups={{0,8,16,24,32,40,48,56,64,72,80,88,96,104,112,120},{1,9,17,25,33,41,49,..., dimensions={0} | all-to-all | bytes 786432 | tf_op jit(solution)/shard_map/all_to_all | solution.py:244
  21.1 16.5 %all_to_all.16 = bf16[8,96,128]{2,1,0:T(8,128)(2,1)S(1)} all-to-all(bf16[8,96,128]{2,1,0:T(8,128)(2,1)S(1)} %broadcast_in_dim.6), channel_id=1, replica_groups=mesh['depth'=2,'row'=16,'col'=8] {'col'}, dimensions={0} | all-to-all | bytes 393216 | tf_op jit(solution)/shard_map/all_to_all | solution.py:258
  37.7 0.1 broadcast_in_dim.7
  37.8 10.0 %all_to_all.17.h0 = bf16[4,640,128]{2,1,0:T(8,128)(2,1)S(1)} all-to-all(bf16[4,640,128]{2,1,0:T(8,128)(2,1)S(1)} %broadcast_in_dim.7), channel_id=1, replica_groups={{0,32,64,96},{8,40,72,104},{16,48,80,112},{24,56,88,120},{1,33,65,97},{..., dimensions={0} | all-to-all | bytes 1310720 | tf_op jit(solution)/shard_map/all_to_all | solution.py:244
  47.8 0.7 collective-permute-start.3
  48.6 4.8 %collective-permute-start.4 = (bf16[2,2,3,128,512]{4,3,2,1,0:T(8,128)(2,1)}, bf16[2,2,3,128,512]{4,3,2,1,0:T(8,128)(2,1)}, u32[]{:S(2)}, u32[]{:S(2)}) collective-permute-start(bf16[2,2,3,128,512]{4,3,2,1,0:T(8,128)(2,1)} %own_ref.1), channel_id=1, source_target_pairs={{0,128},{128,0},{1,129},{129,1},{2,130},{130,2},{3,131},{131,3},{4... | collective-permute-start | bytes 4718600 | tf_op jit(solution)/shard_map/ppermute | solution.py:254
  53.3 1.2 %collective-permute-start.2 = (bf16[4,640,128]{2,1,0:T(8,128)(2,1)S(1)}, bf16[4,640,128]{2,1,0:T(8,128)(2,1)S(1)}, u32[]{:S(2)}, u32[]{:S(2)}) collective-permute-start(bf16[4,640,128]{2,1,0:T(8,128)(2,1)S(1)} %all_to_all.17.h0), channel_id=1, source_target_pairs={{0,24},{1,25},{2,26},{3,27},{4,28},{5,29},{6,30},{7,31},{8,0},{9,1... | collective-permute-start | bytes 1966088 | tf_op jit(solution)/shard_map/ppermute | solution.py:261
  54.5 0.3 collective-permute-start.1
  54.8 4.2 %collective-permute-done.3.h3 = bf16[4,640,128]{2,1,0:T(8,128)(2,1)S(1)} collective-permute-done((bf16[4,640,128]{2,1,0:T(8,128)(2,1)S(1)}, bf16[4,640,128]{2,1,0:T(8,128)(2,1)S(1)}, u32[]{:S(2)}, u32[]{:S(2)}) %collective-permute-start.3) | collective-permute-done | bytes 655392 | tf_op jit(solution)/shard_map/ppermute | solution.py:261
  59.1 4.9 %collective-permute-done.2.h2 = bf16[4,640,128]{2,1,0:T(8,128)(2,1)S(1)} collective-permute-done((bf16[4,640,128]{2,1,0:T(8,128)(2,1)S(1)}, bf16[4,640,128]{2,1,0:T(8,128)(2,1)S(1)}, u32[]{:S(2)}, u32[]{:S(2)}) %collective-permute-start.2) | collective-permute-done | bytes 655392 | tf_op jit(solution)/shard_map/ppermute | solution.py:261
  64.0 2.0 %collective-permute-done.1.h1 = bf16[4,640,128]{2,1,0:T(8,128)(2,1)S(1)} collective-permute-done((bf16[4,640,128]{2,1,0:T(8,128)(2,1)S(1)}, bf16[4,640,128]{2,1,0:T(8,128)(2,1)S(1)}, u32[]{:S(2)}, u32[]{:S(2)}) %collective-permute-start.1) | collective-permute-done | bytes 655392 | tf_op jit(solution)/shard_map/ppermute | solution.py:261
  66.1 0.9 %pad_maximum_fusion = bf16[4,4,128,128]{3,2,1,0:T(8,128)(2,1)} fusion(bf16[1,4,128,128]{3,2,1,0:T(8,128)(2,1)S(1)} %slice_bitcast_fusion, bf16[1,4,128,128]{3,2,1,0:T(8,128)(2,1)S(1)} %slice_bitcast_fusion.1, bf16[1,4,128,128]{3,2,1,0:T(8,128)(2,1)S(1)} %slice_bitcast_fusion.2, bf16[1,4,128,128]{3,2,1,0:T(8,128)(2,1)S(1)} %slice_bitcast_fusion.3), kind=kLoop, calls=%fused_computation.1 | loop fusion | flops 786432 | bytes 1048576 | tf_op jit(solution)/shard_map/stack | solution.py:262
  66.9 4.9 %collective-permute-start.5 = (bf16[4,4,128,128]{3,2,1,0:T(8,128)(2,1)}, bf16[4,4,128,128]{3,2,1,0:T(8,128)(2,1)S(1)}, u32[]{:S(2)}, u32[]{:S(2)}) collective-permute-start(bf16[4,4,128,128]{3,2,1,0:T(8,128)(2,1)} %pad_maximum_fusion), channel_id=1, source_target_pairs={{0,128},{128,0},{1,129},{129,1},{2,130},{130,2},{3,131},{131,3},{4... | collective-permute-start | bytes 1572872 | tf_op jit(solution)/shard_map/ppermute | solution.py:262
  71.9 0.1 pad_add_fusion.where_ref
  71.9 0.0 collective-permute-done.4.swap_ref
  71.9 5.8 %shard_map.37 = (bf16[1024,1024]{1,0:T(8,128)(2,1)S(1)}, f32[4,2,6,128,128]{4,3,2,1,0:T(8,128)S(1)}, f32[512,1024]{1,0:T(8,128)S(1)}, bf16[512,1024]{1,0:T(8,128)(2,1)S(1)}, bf16[6,128,1024]{2,1,0:T(8,128)(2,1)S(1)}) custom-call(s32[2]{0:T(128)S(1)} %pad_add_fusion.where_ref, bf16[4,640,128]{2,1,0:T(8,128)(2,1)S(1)} %all_to_all.17.h0, ...), custom_call_target="tpu_custom_call" | custom-call | flops 3000000000 | bytes 7500000 | tf_op jit(solution)/shard_map/pallas_call | solution.py:191
  77.8 0.0 collective-permute-done.5.other_ref
  77.8 5.9 %shard_map.38 = f32[2,6,128,512]{3,2,1,0:T(8,128)} custom-call(s32[2]{0:T(128)S(1)} %pad_add_fusion.where_ref, bf16[1024,1024]{1,0:T(8,128)(2,1)S(1)} %get-tuple-element.10.sol0, f32[4,2,6,128,128]{4,3,2,1,0:T(8,128)S(1)} %get-tuple-element.11.state, f32[512,1024]{1,0:T(8,128)S(1)} %get-tuple-element.12.left, bf16[512,1024]{1,0:T(8,128)(2,1)S(1)} %get-tuple-element.13.inv, ...), custom_call_target="tpu_custom_call" | custom-call | flops 3000000000 | bytes 7500000 | tf_op jit(solution)/shard_map/pallas_call | solution.py:191
  (13 shorter events, 0.2 us)
Async XLA Ops:
  0.9 4.5 %collective-permute-start = (bf16[128,512]{1,0:T(8,128)(2,1)S(1)}, bf16[128,512]{1,0:T(8,128)(2,1)S(1)}, u32[]{:S(2)}, u32[]{:S(2)}) collective-permute-start(bf16[128,512]{1,0:T(8,128)(2,1)S(1)} %slice_bitcast_fusion.4), channel_id=1, source_target_pairs={{0,128},{128,0},{1,129},{129,1},{2,130},{130,2},{3,131},{131,3},{4... | collective-permute-start | bytes 393224 | tf_op jit(solution)/shard_map/ppermute | solution.py:252
  47.8 11.2 %collective-permute-start.3 = (bf16[4,640,128]{2,1,0:T(8,128)(2,1)S(1)}, bf16[4,640,128]{2,1,0:T(8,128)(2,1)S(1)}, u32[]{:S(2)}, u32[]{:S(2)}) collective-permute-start(bf16[4,640,128]{2,1,0:T(8,128)(2,1)S(1)} %all_to_all.17.h0), channel_id=1, source_target_pairs={{0,16},{1,17},{2,18},{3,19},{4,20},{5,21},{6,22},{7,23},{8,24},{9,... | collective-permute-start | bytes 1966088 | tf_op jit(solution)/shard_map/ppermute | solution.py:261
  48.6 23.4 %collective-permute-start.4 = (bf16[2,2,3,128,512]{4,3,2,1,0:T(8,128)(2,1)}, bf16[2,2,3,128,512]{4,3,2,1,0:T(8,128)(2,1)}, u32[]{:S(2)}, u32[]{:S(2)}) collective-permute-start(bf16[2,2,3,128,512]{4,3,2,1,0:T(8,128)(2,1)} %own_ref.1), channel_id=1, source_target_pairs={{0,128},{128,0},{1,129},{129,1},{2,130},{130,2},{3,131},{131,3},{4... | collective-permute-start | bytes 4718600 | tf_op jit(solution)/shard_map/ppermute | solution.py:254
  53.3 10.7 %collective-permute-start.2 = (bf16[4,640,128]{2,1,0:T(8,128)(2,1)S(1)}, bf16[4,640,128]{2,1,0:T(8,128)(2,1)S(1)}, u32[]{:S(2)}, u32[]{:S(2)}) collective-permute-start(bf16[4,640,128]{2,1,0:T(8,128)(2,1)S(1)} %all_to_all.17.h0), channel_id=1, source_target_pairs={{0,24},{1,25},{2,26},{3,27},{4,28},{5,29},{6,30},{7,31},{8,0},{9,1... | collective-permute-start | bytes 1966088 | tf_op jit(solution)/shard_map/ppermute | solution.py:261
  54.5 11.5 %collective-permute-start.1 = (bf16[4,640,128]{2,1,0:T(8,128)(2,1)S(1)}, bf16[4,640,128]{2,1,0:T(8,128)(2,1)S(1)}, u32[]{:S(2)}, u32[]{:S(2)}) collective-permute-start(bf16[4,640,128]{2,1,0:T(8,128)(2,1)S(1)} %all_to_all.17.h0), channel_id=1, source_target_pairs={{0,8},{1,9},{2,10},{3,11},{4,12},{5,13},{6,14},{7,15},{8,16},{9,17... | collective-permute-start | bytes 1966088 | tf_op jit(solution)/shard_map/ppermute | solution.py:261
  66.9 10.8 %collective-permute-start.5 = (bf16[4,4,128,128]{3,2,1,0:T(8,128)(2,1)}, bf16[4,4,128,128]{3,2,1,0:T(8,128)(2,1)S(1)}, u32[]{:S(2)}, u32[]{:S(2)}) collective-permute-start(bf16[4,4,128,128]{3,2,1,0:T(8,128)(2,1)} %pad_maximum_fusion), channel_id=1, source_target_pairs={{0,128},{128,0},{1,129},{129,1},{2,130},{130,2},{3,131},{131,3},{4... | collective-permute-start | bytes 1572872 | tf_op jit(solution)/shard_map/ppermute | solution.py:262

commit v3 on v2

v3 whole, which is shorter than its diff:
```python
import jax
import jax.numpy as jnp
from jax import lax
from jax.experimental import pallas as pl
from jax.experimental.pallas import tpu as pltpu
from jax.sharding import PartitionSpec as P

BF = jnp.bfloat16
F32 = jnp.float32
SWAP = [(0, 1), (1, 0)]
AXES = ("depth", "row", "col")
SIDE = 4
SHIFTS = (0, 1, 3, 2)
TILES = 4


def place(depth, x, y, z):
    return (depth * 16 + (x % SIDE) * SIDE + y % SIDE) * 8 + z


def plane_groups():
    return [
        [place(d, c // 4, c % 4, z) if d == 0 else place(d, c % 4, c // 4, z) for c in range(16)] for d in range(2) for z in range(8)
    ]


def slow_groups():
    return [
        [place(d, m, o, z) if d == 0 else place(d, o, m, z) for m in range(4)] for d in range(2) for z in range(8) for o in range(4)
    ]


def fast_shift(by):
    return [
        (place(d, x, y, z), place(d, x, y + by, z) if d == 0 else place(d, x + by, y, z))
        for d in range(2)
        for x in range(4)
        for y in range(4)
        for z in range(8)
    ]


def dot(left, right):
    return jnp.dot(left, right, preferred_element_type=F32)


def fill(copies, sems, start=0):
    copies = [pltpu.make_async_copy(source, target, sems.at[start + i]) for i, (source, target) in enumerate(copies)]
    for copy in copies:
        copy.start()
    return copies


def matrix(s, inv_ref, inv):
    return [(inv_ref.at[s, part, :, 256 * k : 256 * k + 256], inv.at[:, 512 * k + 256 * part : 512 * k + 256 * part + 256]) for k in range(2) for part in range(2)]


def half_panel(s, ref, panel):
    return [(ref.at[s, part], panel.at[:, :, 512 * part : 512 * part + 512]) for part in range(2)]


def places(where_ref):
    depth, position = where_ref[0], where_ref[1]
    place_x, place_y = position >> 5, (position >> 3) & 3
    group = jnp.where(depth == 0, place_y, place_x)
    return depth, position, group, place_x + place_y - group


def put(ref, at, back, value):
    rows, columns = value.shape
    for j in range(0, columns, 256):
        real, imag = value[:, j : j + 128], value[:, j + 128 : j + 256]
        ref[at : at + rows, j : j + 128] = real
        ref[at : at + rows, j + 128 : j + 256] = imag
        ref[back : back + rows, j : j + 128] = -imag
        ref[back : back + rows, j + 128 : j + 256] = real


def block(held, s, k):
    return jnp.concatenate(
        [
            jnp.concatenate(
                [ref[m, ((4 * s + zz) * 2 + part) * 32 : ((4 * s + zz) * 2 + part) * 32 + 32, :] for zz in (2 * k, 2 * k + 1) for m in range(4)], axis=0
            )
            for ref in held
            for part in range(2)
        ],
        axis=1,
    )


def solve(inv, work, sol, piece, rows):
    value = dot(inv[:, 0:512], work[0:512])
    low = value[256:] + dot(inv[256:, 512:1024], work[512:1024])
    for at, part in ((0, value[:256]), (256, low)):
        put(sol, at, 512 + at, part.astype(BF))

        @pl.when((rows >> 8) == (at >> 8))
        def _():
            piece[...] = jnp.where((rows & 128) == 0, part[:128], part[128:])


def fill_diag(diag, halves, first):
    for half, shift in zip(halves, SHIFTS):
        at = pl.multiple_of(((first + 4 - shift) & 3) * 128, 128)
        for m in range(4):
            for zz in range(4):
                diag[zz * 128 + m * 32 : zz * 128 + m * 32 + 32, pl.ds(at, 128)] = half[m, zz * 32 : zz * 32 + 32, :]


def load_kernel(where_ref, h0, inv_ref, own_ref, rhs_ref, inv0, inv1, own0, own1, state, sol, piece, work, sems):
    depth, position, group, _ = places(where_ref)
    first = fill(matrix(0, inv_ref, inv0) + half_panel(0, own_ref, own0), sems)
    rest = [(rhs_ref.at[:, :, :, lanes(group, shift)], state.at[j]) for j, shift in enumerate(SHIFTS)]
    rest = fill(rest + matrix(1, inv_ref, inv1) + half_panel(1, own_ref, own1), sems, 6)
    for k in range(2):
        put(work, 512 * k, 512 * k + 256, block([h0], 0, k))
    for copy in first:
        copy.wait()
    solve(inv0, work, sol, piece, (position & 3) * 128)
    for copy in rest:
        copy.wait()
    less(state, state, own0, depth * 3, 0, 3, sol[...], 0)


def lanes(group, shift):
    return pl.ds(pl.multiple_of(((group + 4 - shift) & 3) * 128, 128), 128)


def less(new, old, panel, first, at, count, sol, tile):
    total = dot(panel[at : at + count].reshape(128 * count, 1024), sol)
    cycles = pl.ds(first + at, count)
    for j in range(total.shape[1] // 256):
        for part in range(2):
            place = 256 * j + 128 * part
            new[tile + j, part, cycles] = old[tile + j, part, cycles] - total[:, place : place + 128].reshape(count, 128, 128)


def first_kernel(where_ref, h0, h1, h2, h3, inv0, own0, old, known, known_piece, swap_ref, sol, state, left, swap1, swap0, diag, work, piece, sems):
    depth, position, group, _ = places(where_ref)
    held = (h0, h1, h2, h3)
    loads = fill(half_panel(0, swap_ref, swap0) + half_panel(1, swap_ref, swap1), sems)
    for k in range(2):
        put(work, 512 * k, 512 * k + 256, block(held[1:], 0, k))
    fill_diag(diag, [ref.at[:, 512:640] for ref in held], group)
    solve(inv0, work, sol.at[:, 256:], piece, (position & 3) * 128)
    sol[:, :256] = known[...]
    ours = pl.ds(pl.multiple_of(depth * 512, 512), 512)
    for k in range(2):
        left[256 * k : 256 * k + 256] = block(held, 1, k).astype(F32) - dot(diag[256 * k : 256 * k + 256], sol[ours])
    less(state, old, own0, depth * 3, 0, 3, sol[:, 256:], 1)
    state[0, :, pl.ds(depth * 3, 3)] = old[0, :, pl.ds(depth * 3, 3)]
    for load in loads:
        load.wait()
    less(state, old, swap0, 3 - depth * 3, 0, 3, sol[...], 0)

    @pl.when(position < 4)
    def _():
        for j in range(TILES):
            for part in range(2):
                at = 256 * j + 128 * part
                state[j, part, 0] = known_piece[:, at : at + 128] if j == 0 else piece[:, at - 256 : at - 128]


def second_kernel(where_ref, sol0, state, left, inv, own, swap, half, out_ref, diag, work, sol, piece, new, out_sems):
    depth, position, group, other_group = places(where_ref)
    fill_diag(diag, [half.at[j] for j in range(TILES)], other_group)
    theirs = pl.ds(pl.multiple_of((1 - depth) * 512, 512), 512)
    for k in range(2):
        put(work, 512 * k, 512 * k + 256, (left[256 * k : 256 * k + 256] - dot(diag[256 * k : 256 * k + 256], sol0[theirs])).astype(BF))
    solve(inv, work, sol, piece, (position & 3) * 128)
    stores = []
    for panel, first, at, count in ((own, depth * 3, 0, 2), (own, depth * 3, 2, 1), (swap, 3 - depth * 3, 0, 2), (swap, 3 - depth * 3, 2, 1)):
        less(new, state, panel, first, at, count, sol[...], 0)
        if at == 0:
            @pl.when((position < 8) & (first == 0))
            def _():
                for j in range(TILES):
                    for part in range(2):
                        place = 256 * j + 128 * part
                        new[j, part, 0] = jnp.where(position < 4, state[j, part, 0], piece[:, place : place + 128])

        cycles = pl.ds(first + at, count)
        stores += fill([(new.at[j, :, cycles], out_ref.at[:, cycles, :, lanes(group, shift)]) for j, shift in enumerate(SHIFTS)], out_sems, len(stores))
    for store in stores:
        store.wait()


def update(where, inverses, own, swap, rhs, held, other):
    smem = pl.BlockSpec(memory_space=pltpu.SMEM)
    hbm = pl.BlockSpec(memory_space=pl.ANY)
    vmem = pl.BlockSpec(memory_space=pltpu.VMEM)

    def call(body, cost, out_shape, scratch, *operands):
        return pl.pallas_call(
            body,
            in_specs=[smem] + [vmem if isinstance(value, list) else hbm for value in operands],
            out_specs=[vmem if isinstance(shape, pl.MemoryRef) else hbm for shape in out_shape],
            out_shape=out_shape,
            scratch_shapes=scratch,
            compiler_params=pltpu.CompilerParams(vmem_limit_bytes=14 * 1024 * 1024),
            cost_estimate=pl.CostEstimate(flops=cost, bytes_accessed=cost // 400, transcendentals=0),
        )(where, *[pltpu.with_memory_space_constraint(value[0], pltpu.VMEM) if isinstance(value, list) else value for value in operands])

    inverses, own, swap, rhs = [pltpu.with_memory_space_constraint(value, pltpu.HBM) for value in (inverses, own, swap, rhs)]
    inverse, half = pltpu.VMEM((512, 1024), BF), pltpu.VMEM((3, 128, 1024), BF)
    state = pltpu.VMEM((TILES, 2, 6, 128, 128), F32)
    inv0, inv1, own0, own1, old, known, piece = call(
        load_kernel,
        1_000_000_000,
        [inverse, inverse, half, half, state, pltpu.VMEM((1024, 256), BF), pltpu.VMEM((128, 256), F32)],
        [pltpu.VMEM((1024, 256), BF), pltpu.SemaphoreType.DMA((16,))],
        [held[0]],
        inverses,
        own,
        rhs,
    )
    sol, new, left, swap1 = call(
        first_kernel,
        60_000_000_000,
        [pltpu.VMEM((1024, 1024), BF), state, pltpu.VMEM((512, 1024), F32), half],
        [
            half,
            pltpu.VMEM((512, 512), BF),
            pltpu.VMEM((1024, 768), BF),
            pltpu.VMEM((128, 768), F32),
            pltpu.SemaphoreType.DMA((4,)),
        ],
        *[[value] for value in (*held, inv0, own0, old, known, piece)],
        swap,
    )
    (out,) = call(
        second_kernel,
        3_000_000_000,
        [jax.ShapeDtypeStruct(rhs.shape, F32)],
        [
            pltpu.VMEM((512, 512), BF),
            pltpu.VMEM((1024, 1024), BF),
            pltpu.VMEM((1024, 1024), BF),
            pltpu.VMEM((128, 1024), F32),
            state,
            pltpu.SemaphoreType.DMA((16,)),
        ],
        *[[value] for value in (sol, new, left, inv1, own1, swap1, other)],
    )
    return out


def all_to_all(value, groups):
    return lax.all_to_all(value, AXES, 0, 0, axis_index_groups=groups, tiled=True)


def per_device(rhs, panels, inverses):
    depth = lax.axis_index("depth")
    position = lax.axis_index(("row", "col"))
    where = jnp.stack([depth, position]).astype(jnp.int32)
    swap = lax.ppermute(panels, "depth", SWAP)
    mine = jnp.where(where[0] == 0, panels[0, 0, 0], swap[0, 1, 0])
    rows = rhs[:, 0].astype(BF).reshape(2, 4, 32, 4, 128).transpose(1, 3, 0, 2, 4).reshape(16, 64, 128)
    mine = mine.reshape(4, 32, 4, 128).transpose(0, 2, 1, 3).reshape(16, 32, 128)
    dealt = all_to_all(jnp.concatenate([rows, mine], axis=1), plane_groups())[0]
    line = lax.all_to_all(jnp.broadcast_to(dealt, (8, 96, 128)), "col", 0, 0, tiled=True)
    share = jnp.concatenate([line[:, :64].reshape(512, 128), line[4:, 64:].reshape(128, 128)], axis=0)
    held = all_to_all(jnp.broadcast_to(share, (4, 640, 128)), slow_groups())
    parts = [held] + [lax.ppermute(held, AXES, fast_shift(shift)) for shift in SHIFTS[1:]]
    other = lax.ppermute(jnp.stack([part[:, 512:] for part in parts]), "depth", SWAP)
    return update(where, inverses, panels, swap, rhs, parts, other)


def solution(mesh):
    return jax.shard_map(
        per_device,
        mesh=mesh,
        in_specs=(
            P(None, None, ("row", "col"), "depth"),
            P(None, None, "depth", ("row", "col"), None),
            P(),
        ),
        out_specs=P(None, None, ("row", "col"), "depth"),
        check_vma=False,
    )
```

time: 84 us -> 83 us (0.988)
  starting transfers between devices: 15.2 us -> 11.1 us
  Pallas kernels: 11.7 us -> 14.9 us
  waiting for transfers between devices: 11.2 us -> 13.1 us
  local copies, waits for them, and re-layouts: 2.33 us -> 1.42 us
    ppermute x1 -> x0, starting transfers between devices: 3.33 us -> none  [per_device(): passed = lax.ppermute(first[1], 'depth', SWAP)]
    pallas_call x2 -> x3, Pallas kernels: 11.7 us -> 14.9 us  [call(): pl.pallas_call(body, in_specs=[smem] + [vmem if isinstance(value, list) e...]
    ppermute x1, waiting for transfers between devices: 0.01 us -> 2.04 us  [per_device(): swap = lax.ppermute(panels, 'depth', SWAP)]
    ppermute x1, starting transfers between devices: 4.77 us -> 3.24 us  [per_device(): swap = lax.ppermute(panels, 'depth', SWAP)]
    squeeze x1 -> x0, local copies, waits for them, and re-layouts: 0.91 us -> none  [per_device(): passed = lax.ppermute(first[1], 'depth', SWAP)]
  transfers between devices with their start and end apart: 6 -> 5, of which waited for: 3 -> 4; matrix products, arithmetic and copies ran while one was open for 3% -> 2% of each run, Pallas kernels for 7% -> 11%
where the time goes in v3:
time: 83 us; the launch traced here: 82.7 us
  blocking collectives  40.8 us (49%)
  Pallas kernels  14.9 us (18%)
  waiting for transfers between devices  13.1 us (16%)
  starting transfers between devices  11.1 us (13%)
  local copies, waits for them, and re-layouts  1.42 us (2%)
  other arithmetic  1.22 us (1%)
    all_to_all x2, blocking collectives, all_to_all(): lax.all_to_all(value, AXES, 0, 0, axis_index_groups=groups, tiled=True)  24.1 us
    all_to_all x1, blocking collectives, per_device(): lax.all_to_all(jnp.broadcast_to(dealt, (8, 96, 128)), 'col', 0, 0, tiled=...  16.7 us
    pallas_call x3, Pallas kernels, call(): pl.pallas_call(body, in_specs=[smem] + [vmem if isinstance(value, list) e...  14.9 us
    ppermute x3, waiting for transfers between devices, per_device(): lax.ppermute(held, AXES, fast_shift(shift))  11.1 us
    ppermute x1, starting transfers between devices, per_device(): lax.ppermute(jnp.stack([part[:, 512:] for part in parts]), 'depth', SWAP)  5.03 us
    ppermute x1, starting transfers between devices, per_device(): swap = lax.ppermute(panels, 'depth', SWAP)  3.24 us
    ppermute x3, starting transfers between devices, per_device(): lax.ppermute(held, AXES, fast_shift(shift))  2.84 us
    ppermute x1, waiting for transfers between devices, per_device(): swap = lax.ppermute(panels, 'depth', SWAP)  2.04 us
  transfers between devices with their start and end apart: 5, of which 4 were waited for; matrix products, arithmetic and copies ran while one was open for 2% of the time, Pallas kernels for 11%

profile of v3, /device:TPU:1, one launch (start us, length us, event | category | flops | bytes accessed | tf_op | source)
XLA Modules:
  0.0 82.7 jit_solution(15570537994590332959)
XLA Ops:
  0.0 3.2 %collective-permute-start = (bf16[2,2,3,128,512]{4,3,2,1,0:T(8,128)(2,1)}, bf16[2,2,3,128,512]{4,3,2,1,0:T(8,128)(2,1)S(1)}, u32[]{:S(2)}, u32[]{:S(2)}) collective-permute-start(bf16[2,2,3,128,512]{4,3,2,1,0:T(8,128)(2,1)} %own_ref.1), channel_id=1, source_target_pairs={{0,128},{128,0},{1,129},{129,1},{2,130},{130,2},{3,131},{131,3},{4... | collective-permute-start | bytes 4718600 | tf_op jit(solution)/shard_map/ppermute | solution.py:257
  3.2 1.1 %slice.58 = bf16[2,1,128,512]{3,2,1,0:T(8,128)(2,1)S(1)} slice(f32[2,6,128,512]{3,2,1,0:T(8,128)} %rhs_ref.1), slice={[0:2], [0:1], [0:128], [0:512]} | slice | bytes 524288 | tf_op jit(solution)/shard_map/slice | solution.py:259
  4.3 0.1 convert_element_type.5
  4.4 2.0 %collective-permute-done.swap_ref = bf16[2,2,3,128,512]{4,3,2,1,0:T(8,128)(2,1)S(1)} collective-permute-done((bf16[2,2,3,128,512]{4,3,2,1,0:T(8,128)(2,1)}, bf16[2,2,3,128,512]{4,3,2,1,0:T(8,128)(2,1)S(1)}, u32[]{:S(2)}, u32[]{:S(2)}) %collective-permute-start) | collective-permute-done | bytes 1572896 | tf_op jit(solution)/shard_map/ppermute | solution.py:257
  6.5 0.0 copy-start
  6.5 1.0 %slice_select_fusion = bf16[1,1,1,128,512]{4,3,2,1,0:T(8,128)(2,1)S(1)} fusion(bf16[2,2,3,128,512]{4,3,2,1,0:T(8,128)(2,1)S(1)} %collective-permute-done.swap_ref, bf16[2,2,3,128,512]{4,3,2,1,0:T(8,128)(2,1)} %own_ref.1, pred[]{:T(512)S(6)} %eq.3), kind=kLoop, calls=%fused_computation.8 | loop fusion | flops 65536 | bytes 393217 | tf_op jit(solution)/shard_map/jit(_where)/select_n | solution.py:258
  7.6 14.0 %all_to_all.15 = bf16[16,96,128]{2,1,0:T(8,128)(2,1)S(1)} all-to-all(bf16[16,96,128]{2,1,0:T(8,128)(2,1)S(1)} %pad_maximum_fusion.1), channel_id=1, replica_groups={{0,8,16,24,32,40,48,56,64,72,80,88,96,104,112,120},{1,9,17,25,33,41,49,..., dimensions={0} | all-to-all | bytes 786432 | tf_op jit(solution)/shard_map/all_to_all | solution.py:250
  21.7 16.7 %all_to_all.16 = bf16[8,96,128]{2,1,0:T(8,128)(2,1)S(1)} all-to-all(bf16[8,96,128]{2,1,0:T(8,128)(2,1)S(1)} %broadcast_in_dim.6), channel_id=1, replica_groups=mesh['depth'=2,'row'=16,'col'=8] {'col'}, dimensions={0} | all-to-all | bytes 393216 | tf_op jit(solution)/shard_map/all_to_all | solution.py:262
  38.5 0.1 broadcast_in_dim.7
  38.6 0.0 copy-done
  38.6 10.0 %all_to_all.17.h0 = bf16[4,640,128]{2,1,0:T(8,128)(2,1)S(1)} all-to-all(bf16[4,640,128]{2,1,0:T(8,128)(2,1)S(1)} %broadcast_in_dim.7), channel_id=1, replica_groups={{0,32,64,96},{8,40,72,104},{16,48,80,112},{24,56,88,120},{1,33,65,97},{..., dimensions={0} | all-to-all | bytes 1310720 | tf_op jit(solution)/shard_map/all_to_all | solution.py:250
  48.6 0.7 collective-permute-start.3
  49.3 2.2 %collective-permute-start.2 = (bf16[4,640,128]{2,1,0:T(8,128)(2,1)S(1)}, bf16[4,640,128]{2,1,0:T(8,128)(2,1)S(1)}, u32[]{:S(2)}, u32[]{:S(2)}) collective-permute-start(bf16[4,640,128]{2,1,0:T(8,128)(2,1)S(1)} %all_to_all.17.h0), channel_id=1, source_target_pairs={{0,24},{1,25},{2,26},{3,27},{4,28},{5,29},{6,30},{7,31},{8,0},{9,1... | collective-permute-start | bytes 1966088 | tf_op jit(solution)/shard_map/ppermute | solution.py:265
  51.5 0.1 pad_add_fusion.where_ref
  51.5 0.0 collective-permute-start.1
  51.5 4.2 %shard_map.37 = (bf16[512,1024]{1,0:T(8,128)(2,1)S(1)}, bf16[512,1024]{1,0:T(8,128)(2,1)S(1)}, bf16[3,128,1024]{2,1,0:T(8,128)(2,1)S(1)}, bf16[3,128,1024]{2,1,0...) custom-call(s32[2]{0:T(128)S(1)} %pad_add_fusion.where_ref, ...), custom_call_target="tpu_custom_call" | custom-call | flops 1000000000 | bytes 2500000 | tf_op jit(solution)/shard_map/pallas_call | solution.py:195
  55.8 4.1 %collective-permute-done.3.h3 = bf16[4,640,128]{2,1,0:T(8,128)(2,1)S(1)} collective-permute-done((bf16[4,640,128]{2,1,0:T(8,128)(2,1)S(1)}, bf16[4,640,128]{2,1,0:T(8,128)(2,1)S(1)}, u32[]{:S(2)}, u32[]{:S(2)}) %collective-permute-start.3) | collective-permute-done | bytes 655392 | tf_op jit(solution)/shard_map/ppermute | solution.py:265
  59.9 5.0 %collective-permute-done.2.h2 = bf16[4,640,128]{2,1,0:T(8,128)(2,1)S(1)} collective-permute-done((bf16[4,640,128]{2,1,0:T(8,128)(2,1)S(1)}, bf16[4,640,128]{2,1,0:T(8,128)(2,1)S(1)}, u32[]{:S(2)}, u32[]{:S(2)}) %collective-permute-start.2) | collective-permute-done | bytes 655392 | tf_op jit(solution)/shard_map/ppermute | solution.py:265
  64.9 2.0 %collective-permute-done.1.h1 = bf16[4,640,128]{2,1,0:T(8,128)(2,1)S(1)} collective-permute-done((bf16[4,640,128]{2,1,0:T(8,128)(2,1)S(1)}, bf16[4,640,128]{2,1,0:T(8,128)(2,1)S(1)}, u32[]{:S(2)}, u32[]{:S(2)}) %collective-permute-start.1) | collective-permute-done | bytes 655392 | tf_op jit(solution)/shard_map/ppermute | solution.py:265
  66.9 0.1 pad_maximum_fusion
  67.0 5.0 %collective-permute-start.4 = (bf16[4,4,128,128]{3,2,1,0:T(8,128)(2,1)S(1)}, bf16[4,4,128,128]{3,2,1,0:T(8,128)(2,1)S(1)}, u32[]{:S(2)}, u32[]{:S(2)}) collective-permute-start(bf16[4,4,128,128]{3,2,1,0:T(8,128)(2,1)S(1)} %pad_maximum_fusion), channel_id=1, source_target_pairs={{0,128},{128,0},{1,129},{129,1},{2,130},{130,2},{3,131},{131,3},{4... | collective-permute-start | bytes 1572872 | tf_op jit(solution)/shard_map/ppermute | solution.py:266
  72.0 4.8 %shard_map.38 = (bf16[1024,1024]{1,0:T(8,128)(2,1)S(1)}, f32[4,2,6,128,128]{4,3,2,1,0:T(8,128)S(1)}, f32[512,1024]{1,0:T(8,128)S(1)}, bf16[3,128,1024]{2,1,0:T(8,128)(2,1)S(1)}) custom-call(s32[2]{0:T(128)S(1)} %pad_add_fusion.where_ref, bf16[4,640,128]{2,1,0:T(8,128)(2,1)S(1)} %all_to_all.17.h0, bf16[4,640,128]{2,1,0:T(8,128)(2,1)S(1)} %collective-permute-done.1.h1, ...), custom_call_target="tpu_custom_call" | custom-call | flops 60000002048 | bytes 150000000 | tf_op jit(solution)/shard_map/pallas_call | solution.py:195
  76.8 0.0 collective-permute-done.4.half
  76.8 5.9 %shard_map.39 = f32[2,6,128,512]{3,2,1,0:T(8,128)} custom-call(s32[2]{0:T(128)S(1)} %pad_add_fusion.where_ref, bf16[1024,1024]{1,0:T(8,128)(2,1)S(1)} %get-tuple-element.21.sol0, f32[4,2,6,128,128]{4,3,2,1,0:T(8,128)S(1)} %get-tuple-element.22.state, f32[512,1024]{1,0:T(8,128)S(1)} %get-tuple-element.23.left, bf16[512,1024]{1,0:T(8,128)(2,1)S(1)} %get-tuple-element.24.inv, ...), custom_call_target="tpu_custom_call" | custom-call | flops 3000000000 | bytes 7500000 | tf_op jit(solution)/shard_map/pallas_call | solution.py:195
  (13 shorter events, 0.2 us)
Async XLA Ops:
  0.0 6.5 %collective-permute-start = (bf16[2,2,3,128,512]{4,3,2,1,0:T(8,128)(2,1)}, bf16[2,2,3,128,512]{4,3,2,1,0:T(8,128)(2,1)S(1)}, u32[]{:S(2)}, u32[]{:S(2)}) collective-permute-start(bf16[2,2,3,128,512]{4,3,2,1,0:T(8,128)(2,1)} %own_ref.1), channel_id=1, source_target_pairs={{0,128},{128,0},{1,129},{129,1},{2,130},{130,2},{3,131},{131,3},{4... | collective-permute-start | bytes 4718600 | tf_op jit(solution)/shard_map/ppermute | solution.py:257
  6.5 32.1 %copy-start = (bf16[2,2,3,128,512]{4,3,2,1,0:T(8,128)(2,1)}, bf16[2,2,3,128,512]{4,3,2,1,0:T(8,128)(2,1)S(1)}, u32[]{:S(2)}) copy-start(bf16[2,2,3,128,512]{4,3,2,1,0:T(8,128)(2,1)S(1)} %collective-permute-done.swap_ref) | copy-start | bytes 4718596
  48.6 11.2 %collective-permute-start.3 = (bf16[4,640,128]{2,1,0:T(8,128)(2,1)S(1)}, bf16[4,640,128]{2,1,0:T(8,128)(2,1)S(1)}, u32[]{:S(2)}, u32[]{:S(2)}) collective-permute-start(bf16[4,640,128]{2,1,0:T(8,128)(2,1)S(1)} %all_to_all.17.h0), channel_id=1, source_target_pairs={{0,16},{1,17},{2,18},{3,19},{4,20},{5,21},{6,22},{7,23},{8,24},{9,... | collective-permute-start | bytes 1966088 | tf_op jit(solution)/shard_map/ppermute | solution.py:265
  49.3 15.6 %collective-permute-start.2 = (bf16[4,640,128]{2,1,0:T(8,128)(2,1)S(1)}, bf16[4,640,128]{2,1,0:T(8,128)(2,1)S(1)}, u32[]{:S(2)}, u32[]{:S(2)}) collective-permute-start(bf16[4,640,128]{2,1,0:T(8,128)(2,1)S(1)} %all_to_all.17.h0), channel_id=1, source_target_pairs={{0,24},{1,25},{2,26},{3,27},{4,28},{5,29},{6,30},{7,31},{8,0},{9,1... | collective-permute-start | bytes 1966088 | tf_op jit(solution)/shard_map/ppermute | solution.py:265
  51.5 15.3 %collective-permute-start.1 = (bf16[4,640,128]{2,1,0:T(8,128)(2,1)S(1)}, bf16[4,640,128]{2,1,0:T(8,128)(2,1)S(1)}, u32[]{:S(2)}, u32[]{:S(2)}) collective-permute-start(bf16[4,640,128]{2,1,0:T(8,128)(2,1)S(1)} %all_to_all.17.h0), channel_id=1, source_target_pairs={{0,8},{1,9},{2,10},{3,11},{4,12},{5,13},{6,14},{7,15},{8,16},{9,17... | collective-permute-start | bytes 1966088 | tf_op jit(solution)/shard_map/ppermute | solution.py:265
  67.0 9.8 %collective-permute-start.4 = (bf16[4,4,128,128]{3,2,1,0:T(8,128)(2,1)S(1)}, bf16[4,4,128,128]{3,2,1,0:T(8,128)(2,1)S(1)}, u32[]{:S(2)}, u32[]{:S(2)}) collective-permute-start(bf16[4,4,128,128]{3,2,1,0:T(8,128)(2,1)S(1)} %pad_maximum_fusion), channel_id=1, source_target_pairs={{0,128},{128,0},{1,129},{129,1},{2,130},{130,2},{3,131},{131,3},{4... | collective-permute-start | bytes 1572872 | tf_op jit(solution)/shard_map/ppermute | solution.py:266

commit v4 on v3

--- a/solution.py
+++ b/solution.py
@@ -108,11 +108,11 @@
                 diag[zz * 128 + m * 32 : zz * 128 + m * 32 + 32, pl.ds(at, 128)] = half[m, zz * 32 : zz * 32 + 32, :]
 
 
-def load_kernel(where_ref, h0, inv_ref, own_ref, rhs_ref, inv0, inv1, own0, own1, state, sol, piece, work, sems):
+def load_kernel(where_ref, h0, inv_ref, own_ref, swap_ref, rhs_ref, inv0, inv1, own, swap, state, sol, piece, work, sems):
     depth, position, group, _ = places(where_ref)
-    first = fill(matrix(0, inv_ref, inv0) + half_panel(0, own_ref, own0), sems)
+    first = fill(matrix(0, inv_ref, inv0) + half_panel(0, own_ref, own.at[0]) + half_panel(0, swap_ref, swap.at[0]), sems)
     rest = [(rhs_ref.at[:, :, :, lanes(group, shift)], state.at[j]) for j, shift in enumerate(SHIFTS)]
-    rest = fill(rest + matrix(1, inv_ref, inv1) + half_panel(1, own_ref, own1), sems, 6)
+    rest = fill(rest + matrix(1, inv_ref, inv1) + half_panel(1, own_ref, own.at[1]) + half_panel(1, swap_ref, swap.at[1]), sems, 8)
     for k in range(2):
         put(work, 512 * k, 512 * k + 256, block([h0], 0, k))
     for copy in first:
@@ -120,7 +120,8 @@
     solve(inv0, work, sol, piece, (position & 3) * 128)
     for copy in rest:
         copy.wait()
-    less(state, state, own0, depth * 3, 0, 3, sol[...], 0)
+    less(state, state, own.at[0], depth * 3, 0, 3, sol[...], 0)
+    less(state, state, swap.at[0], 3 - depth * 3, 0, 3, sol[...], 0)
 
 
 def lanes(group, shift):
@@ -136,10 +137,9 @@
             new[tile + j, part, cycles] = old[tile + j, part, cycles] - total[:, place : place + 128].reshape(count, 128, 128)
 
 
-def first_kernel(where_ref, h0, h1, h2, h3, inv0, own0, old, known, known_piece, swap_ref, sol, state, left, swap1, swap0, diag, work, piece, sems):
+def first_kernel(where_ref, h0, h1, h2, h3, inv0, own, swap, old, known, known_piece, sol, state, left, diag, work, piece):
     depth, position, group, _ = places(where_ref)
     held = (h0, h1, h2, h3)
-    loads = fill(half_panel(0, swap_ref, swap0) + half_panel(1, swap_ref, swap1), sems)
     for k in range(2):
         put(work, 512 * k, 512 * k + 256, block(held[1:], 0, k))
     fill_diag(diag, [ref.at[:, 512:640] for ref in held], group)
@@ -148,11 +148,9 @@
     ours = pl.ds(pl.multiple_of(depth * 512, 512), 512)
     for k in range(2):
         left[256 * k : 256 * k + 256] = block(held, 1, k).astype(F32) - dot(diag[256 * k : 256 * k + 256], sol[ours])
-    less(state, old, own0, depth * 3, 0, 3, sol[:, 256:], 1)
-    state[0, :, pl.ds(depth * 3, 3)] = old[0, :, pl.ds(depth * 3, 3)]
-    for load in loads:
-        load.wait()
-    less(state, old, swap0, 3 - depth * 3, 0, 3, sol[...], 0)
+    state[0] = old[0]
+    less(state, old, own.at[0], depth * 3, 0, 3, sol[:, 256:], 1)
+    less(state, old, swap.at[0], 3 - depth * 3, 0, 3, sol[:, 256:], 1)
 
     @pl.when(position < 4)
     def _():
@@ -171,7 +169,7 @@
     solve(inv, work, sol, piece, (position & 3) * 128)
     stores = []
     for panel, first, at, count in ((own, depth * 3, 0, 2), (own, depth * 3, 2, 1), (swap, 3 - depth * 3, 0, 2), (swap, 3 - depth * 3, 2, 1)):
-        less(new, state, panel, first, at, count, sol[...], 0)
+        less(new, state, panel.at[1], first, at, count, sol[...], 0)
         if at == 0:
             @pl.when((position < 8) & (first == 0))
             def _():
@@ -203,31 +201,29 @@
         )(where, *[pltpu.with_memory_space_constraint(value[0], pltpu.VMEM) if isinstance(value, list) else value for value in operands])
 
     inverses, own, swap, rhs = [pltpu.with_memory_space_constraint(value, pltpu.HBM) for value in (inverses, own, swap, rhs)]
-    inverse, half = pltpu.VMEM((512, 1024), BF), pltpu.VMEM((3, 128, 1024), BF)
+    inverse, half = pltpu.VMEM((512, 1024), BF), pltpu.VMEM((2, 3, 128, 1024), BF)
     state = pltpu.VMEM((TILES, 2, 6, 128, 128), F32)
-    inv0, inv1, own0, own1, old, known, piece = call(
+    inv0, inv1, own, swap, old, known, piece = call(
         load_kernel,
         1_000_000_000,
         [inverse, inverse, half, half, state, pltpu.VMEM((1024, 256), BF), pltpu.VMEM((128, 256), F32)],
-        [pltpu.VMEM((1024, 256), BF), pltpu.SemaphoreType.DMA((16,))],
+        [pltpu.VMEM((1024, 256), BF), pltpu.SemaphoreType.DMA((20,))],
         [held[0]],
         inverses,
         own,
+        swap,
         rhs,
     )
-    sol, new, left, swap1 = call(
+    sol, new, left = call(
         first_kernel,
         60_000_000_000,
-        [pltpu.VMEM((1024, 1024), BF), state, pltpu.VMEM((512, 1024), F32), half],
+        [pltpu.VMEM((1024, 1024), BF), state, pltpu.VMEM((512, 1024), F32)],
         [
-            half,
             pltpu.VMEM((512, 512), BF),
             pltpu.VMEM((1024, 768), BF),
             pltpu.VMEM((128, 768), F32),
-            pltpu.SemaphoreType.DMA((4,)),
         ],
-        *[[value] for value in (*held, inv0, own0, old, known, piece)],
-        swap,
+        *[[value] for value in (*held, inv0, own, swap, old, known, piece)],
     )
     (out,) = call(
         second_kernel,
@@ -241,7 +237,7 @@
             state,
             pltpu.SemaphoreType.DMA((16,)),
         ],
-        *[[value] for value in (sol, new, left, inv1, own1, swap1, other)],
+        *[[value] for value in (sol, new, left, inv1, own, swap, other)],
     )
     return out
 
@@ -255,7 +251,7 @@
     position = lax.axis_index(("row", "col"))
     where = jnp.stack([depth, position]).astype(jnp.int32)
     swap = lax.ppermute(panels, "depth", SWAP)
-    mine = jnp.where(where[0] == 0, panels[0, 0, 0], swap[0, 1, 0])
+    mine = jnp.where(where[0] == 0, lax.optimization_barrier(panels[0, 0, 0]), swap[0, 1, 0])
     rows = rhs[:, 0].astype(BF).reshape(2, 4, 32, 4, 128).transpose(1, 3, 0, 2, 4).reshape(16, 64, 128)
     mine = mine.reshape(4, 32, 4, 128).transpose(0, 2, 1, 3).reshape(16, 32, 128)
     dealt = all_to_all(jnp.concatenate([rows, mine], axis=1), plane_groups())[0]

time: 83 us -> 81.4 us (0.981)
  waiting for transfers between devices: 13.1 us -> 11.6 us
  other arithmetic: 1.22 us -> 0.2 us
  local copies, waits for them, and re-layouts: 1.42 us -> 2.34 us
    select_n x1, other arithmetic: 1.04 us -> 0.02 us  [per_device(): jnp.where(where[0] == 0, lax.optimization_barrier(panels[0, 0, 0]), swap[...]
    ppermute x1, waiting for transfers between devices: 2.04 us -> 1.12 us  [per_device(): swap = lax.ppermute(panels, 'depth', SWAP)]
    squeeze x0 -> x1, local copies, waits for them, and re-layouts: none -> 0.91 us  [per_device(): panels[0, 0, 0]]
  transfers between devices with their start and end apart: 5 -> 5, of which waited for: 4 -> 4; matrix products, arithmetic and copies ran while one was open for 2% -> 3% of each run, Pallas kernels for 11% -> 11%
where the time goes in v4:
time: 81.4 us; the launch traced here: 81.1 us
  blocking collectives  40.8 us (50%)
  Pallas kernels  14.9 us (18%)
  waiting for transfers between devices  11.6 us (14%)
  starting transfers between devices  11.1 us (14%)
  local copies, waits for them, and re-layouts  2.34 us (3%)
    all_to_all x2, blocking collectives, all_to_all(): lax.all_to_all(value, AXES, 0, 0, axis_index_groups=groups, tiled=True)  24.1 us
    all_to_all x1, blocking collectives, per_device(): lax.all_to_all(jnp.broadcast_to(dealt, (8, 96, 128)), 'col', 0, 0, tiled=...  16.7 us
    pallas_call x3, Pallas kernels, call(): pl.pallas_call(body, in_specs=[smem] + [vmem if isinstance(value, list) e...  14.9 us
    ppermute x3, waiting for transfers between devices, per_device(): lax.ppermute(held, AXES, fast_shift(shift))  10.5 us
    ppermute x1, starting transfers between devices, per_device(): lax.ppermute(jnp.stack([part[:, 512:] for part in parts]), 'depth', SWAP)  5.03 us
    ppermute x1, starting transfers between devices, per_device(): swap = lax.ppermute(panels, 'depth', SWAP)  3.24 us
    ppermute x3, starting transfers between devices, per_device(): lax.ppermute(held, AXES, fast_shift(shift))  2.84 us
  transfers between devices with their start and end apart: 5, of which 4 were waited for; matrix products, arithmetic and copies ran while one was open for 3% of the time, Pallas kernels for 11%

profile of v4, /device:TPU:1, one launch (start us, length us, event | category | flops | bytes accessed | tf_op | source)
XLA Modules:
  0.0 81.1 jit_solution(15578885701192908573)
XLA Ops:
  0.0 3.2 %collective-permute-start = (bf16[2,2,3,128,512]{4,3,2,1,0:T(8,128)(2,1)}, bf16[2,2,3,128,512]{4,3,2,1,0:T(8,128)(2,1)S(1)}, u32[]{:S(2)}, u32[]{:S(2)}) collective-permute-start(bf16[2,2,3,128,512]{4,3,2,1,0:T(8,128)(2,1)} %own_ref.1), channel_id=1, source_target_pairs={{0,128},{128,0},{1,129},{129,1},{2,130},{130,2},{3,131},{131,3},{4... | collective-permute-start | bytes 4718600 | tf_op jit(solution)/shard_map/ppermute | solution.py:253
  3.2 0.9 %slice_bitcast_fusion.5 = bf16[128,512]{1,0:T(8,128)(2,1)S(1)} fusion(bf16[2,2,3,128,512]{4,3,2,1,0:T(8,128)(2,1)} %own_ref.1), kind=kLoop, calls=%fused_computation.10 | loop fusion | bytes 262144 | tf_op jit(solution)/shard_map/squeeze | solution.py:254
  4.2 1.1 %slice.60 = bf16[2,1,128,512]{3,2,1,0:T(8,128)(2,1)S(1)} slice(f32[2,6,128,512]{3,2,1,0:T(8,128)} %rhs_ref.1), slice={[0:2], [0:1], [0:128], [0:512]} | slice | bytes 524288 | tf_op jit(solution)/shard_map/slice | solution.py:255
  5.2 0.1 convert_element_type.5
  5.4 1.1 %collective-permute-done.swap_ref = bf16[2,2,3,128,512]{4,3,2,1,0:T(8,128)(2,1)S(1)} collective-permute-done((bf16[2,2,3,128,512]{4,3,2,1,0:T(8,128)(2,1)}, bf16[2,2,3,128,512]{4,3,2,1,0:T(8,128)(2,1)S(1)}, u32[]{:S(2)}, u32[]{:S(2)}) %collective-permute-start) | collective-permute-done | bytes 1572896 | tf_op jit(solution)/shard_map/ppermute | solution.py:253
  6.5 0.0 copy-start
  6.6 14.0 %all_to_all.15 = bf16[16,96,128]{2,1,0:T(8,128)(2,1)S(1)} all-to-all(bf16[16,96,128]{2,1,0:T(8,128)(2,1)S(1)} %pad_maximum_fusion.1), channel_id=1, replica_groups={{0,8,16,24,32,40,48,56,64,72,80,88,96,104,112,120},{1,9,17,25,33,41,49,..., dimensions={0} | all-to-all | bytes 786432 | tf_op jit(solution)/shard_map/all_to_all | solution.py:246
  20.7 16.7 %all_to_all.16 = bf16[8,96,128]{2,1,0:T(8,128)(2,1)S(1)} all-to-all(bf16[8,96,128]{2,1,0:T(8,128)(2,1)S(1)} %broadcast_in_dim.6), channel_id=1, replica_groups=mesh['depth'=2,'row'=16,'col'=8] {'col'}, dimensions={0} | all-to-all | bytes 393216 | tf_op jit(solution)/shard_map/all_to_all | solution.py:258
  37.4 0.1 broadcast_in_dim.7
  37.5 0.0 copy-done
  37.6 10.0 %all_to_all.17.h0 = bf16[4,640,128]{2,1,0:T(8,128)(2,1)S(1)} all-to-all(bf16[4,640,128]{2,1,0:T(8,128)(2,1)S(1)} %broadcast_in_dim.7), channel_id=1, replica_groups={{0,32,64,96},{8,40,72,104},{16,48,80,112},{24,56,88,120},{1,33,65,97},{..., dimensions={0} | all-to-all | bytes 1310720 | tf_op jit(solution)/shard_map/all_to_all | solution.py:246
  47.6 0.7 collective-permute-start.3
  48.3 2.2 %collective-permute-start.2 = (bf16[4,640,128]{2,1,0:T(8,128)(2,1)S(1)}, bf16[4,640,128]{2,1,0:T(8,128)(2,1)S(1)}, u32[]{:S(2)}, u32[]{:S(2)}) collective-permute-start(bf16[4,640,128]{2,1,0:T(8,128)(2,1)S(1)} %all_to_all.17.h0), channel_id=1, source_target_pairs={{0,24},{1,25},{2,26},{3,27},{4,28},{5,29},{6,30},{7,31},{8,0},{9,1... | collective-permute-start | bytes 1966088 | tf_op jit(solution)/shard_map/ppermute | solution.py:261
  50.4 0.1 pad_add_fusion.where_ref
  50.5 0.0 collective-permute-start.1
  50.5 4.8 %shard_map.37 = (bf16[512,1024]{1,0:T(8,128)(2,1)S(1)}, bf16[512,1024]{1,0:T(8,128)(2,1)S(1)}, bf16[2,3,128,1024]{3,2,1,0:T(8,128)(2,1)S(1)}, bf16[2,3,128,1024]...) custom-call(s32[2]{0:T(128)S(1)} %pad_add_fusion.where_ref, ...), custom_call_target="tpu_custom_call" | custom-call | flops 1000000000 | bytes 2500000 | tf_op jit(solution)/shard_map/pallas_call | solution.py:193
  55.3 3.5 %collective-permute-done.3.h3 = bf16[4,640,128]{2,1,0:T(8,128)(2,1)S(1)} collective-permute-done((bf16[4,640,128]{2,1,0:T(8,128)(2,1)S(1)}, bf16[4,640,128]{2,1,0:T(8,128)(2,1)S(1)}, u32[]{:S(2)}, u32[]{:S(2)}) %collective-permute-start.3) | collective-permute-done | bytes 655392 | tf_op jit(solution)/shard_map/ppermute | solution.py:261
  58.8 5.0 %collective-permute-done.2.h2 = bf16[4,640,128]{2,1,0:T(8,128)(2,1)S(1)} collective-permute-done((bf16[4,640,128]{2,1,0:T(8,128)(2,1)S(1)}, bf16[4,640,128]{2,1,0:T(8,128)(2,1)S(1)}, u32[]{:S(2)}, u32[]{:S(2)}) %collective-permute-start.2) | collective-permute-done | bytes 655392 | tf_op jit(solution)/shard_map/ppermute | solution.py:261
  63.9 2.0 %collective-permute-done.1.h1 = bf16[4,640,128]{2,1,0:T(8,128)(2,1)S(1)} collective-permute-done((bf16[4,640,128]{2,1,0:T(8,128)(2,1)S(1)}, bf16[4,640,128]{2,1,0:T(8,128)(2,1)S(1)}, u32[]{:S(2)}, u32[]{:S(2)}) %collective-permute-start.1) | collective-permute-done | bytes 655392 | tf_op jit(solution)/shard_map/ppermute | solution.py:261
  65.9 0.1 pad_maximum_fusion
  65.9 5.0 %collective-permute-start.4 = (bf16[4,4,128,128]{3,2,1,0:T(8,128)(2,1)S(1)}, bf16[4,4,128,128]{3,2,1,0:T(8,128)(2,1)S(1)}, u32[]{:S(2)}, u32[]{:S(2)}) collective-permute-start(bf16[4,4,128,128]{3,2,1,0:T(8,128)(2,1)S(1)} %pad_maximum_fusion), channel_id=1, source_target_pairs={{0,128},{128,0},{1,129},{129,1},{2,130},{130,2},{3,131},{131,3},{4... | collective-permute-start | bytes 1572872 | tf_op jit(solution)/shard_map/ppermute | solution.py:262
  71.0 4.2 %shard_map.38 = (bf16[1024,1024]{1,0:T(8,128)(2,1)S(1)}, f32[4,2,6,128,128]{4,3,2,1,0:T(8,128)S(1)}, f32[512,1024]{1,0:T(8,128)S(1)}) custom-call(s32[2]{0:T(128)S(1)} %pad_add_fusion.where_ref, bf16[4,640,128]{2,1,0:T(8,128)(2,1)S(1)} %all_to_all.17.h0, bf16[4,640,128]{2,1,0:T(8,128)(2,1)S(1)} %collective-permute-done.1.h1, ...), custom_call_target="tpu_custom_call" | custom-call | flops 60000002048 | bytes 150000000 | tf_op jit(solution)/shard_map/pallas_call | solution.py:193
  75.2 0.0 collective-permute-done.4.half
  75.2 5.9 %shard_map.39 = f32[2,6,128,512]{3,2,1,0:T(8,128)} custom-call(s32[2]{0:T(128)S(1)} %pad_add_fusion.where_ref, bf16[1024,1024]{1,0:T(8,128)(2,1)S(1)} %get-tuple-element.21.sol0, f32[4,2,6,128,128]{4,3,2,1,0:T(8,128)S(1)} %get-tuple-element.22.state, f32[512,1024]{1,0:T(8,128)S(1)} %get-tuple-element.23.left, bf16[512,1024]{1,0:T(8,128)(2,1)S(1)} %get-tuple-element.24.inv, ...), custom_call_target="tpu_custom_call" | custom-call | flops 3000000000 | bytes 7500000 | tf_op jit(solution)/shard_map/pallas_call | solution.py:193
  (14 shorter events, 0.2 us)
Async XLA Ops:
  0.0 6.5 %collective-permute-start = (bf16[2,2,3,128,512]{4,3,2,1,0:T(8,128)(2,1)}, bf16[2,2,3,128,512]{4,3,2,1,0:T(8,128)(2,1)S(1)}, u32[]{:S(2)}, u32[]{:S(2)}) collective-permute-start(bf16[2,2,3,128,512]{4,3,2,1,0:T(8,128)(2,1)} %own_ref.1), channel_id=1, source_target_pairs={{0,128},{128,0},{1,129},{129,1},{2,130},{130,2},{3,131},{131,3},{4... | collective-permute-start | bytes 4718600 | tf_op jit(solution)/shard_map/ppermute | solution.py:253
  6.5 31.1 %copy-start = (bf16[2,2,3,128,512]{4,3,2,1,0:T(8,128)(2,1)}, bf16[2,2,3,128,512]{4,3,2,1,0:T(8,128)(2,1)S(1)}, u32[]{:S(2)}) copy-start(bf16[2,2,3,128,512]{4,3,2,1,0:T(8,128)(2,1)S(1)} %collective-permute-done.swap_ref) | copy-start | bytes 4718596
  47.6 11.2 %collective-permute-start.3 = (bf16[4,640,128]{2,1,0:T(8,128)(2,1)S(1)}, bf16[4,640,128]{2,1,0:T(8,128)(2,1)S(1)}, u32[]{:S(2)}, u32[]{:S(2)}) collective-permute-start(bf16[4,640,128]{2,1,0:T(8,128)(2,1)S(1)} %all_to_all.17.h0), channel_id=1, source_target_pairs={{0,16},{1,17},{2,18},{3,19},{4,20},{5,21},{6,22},{7,23},{8,24},{9,... | collective-permute-start | bytes 1966088 | tf_op jit(solution)/shard_map/ppermute | solution.py:261
  48.3 15.6 %collective-permute-start.2 = (bf16[4,640,128]{2,1,0:T(8,128)(2,1)S(1)}, bf16[4,640,128]{2,1,0:T(8,128)(2,1)S(1)}, u32[]{:S(2)}, u32[]{:S(2)}) collective-permute-start(bf16[4,640,128]{2,1,0:T(8,128)(2,1)S(1)} %all_to_all.17.h0), channel_id=1, source_target_pairs={{0,24},{1,25},{2,26},{3,27},{4,28},{5,29},{6,30},{7,31},{8,0},{9,1... | collective-permute-start | bytes 1966088 | tf_op jit(solution)/shard_map/ppermute | solution.py:261
  50.5 15.3 %collective-permute-start.1 = (bf16[4,640,128]{2,1,0:T(8,128)(2,1)S(1)}, bf16[4,640,128]{2,1,0:T(8,128)(2,1)S(1)}, u32[]{:S(2)}, u32[]{:S(2)}) collective-permute-start(bf16[4,640,128]{2,1,0:T(8,128)(2,1)S(1)} %all_to_all.17.h0), channel_id=1, source_target_pairs={{0,8},{1,9},{2,10},{3,11},{4,12},{5,13},{6,14},{7,15},{8,16},{9,17... | collective-permute-start | bytes 1966088 | tf_op jit(solution)/shard_map/ppermute | solution.py:261
  65.9 9.2 %collective-permute-start.4 = (bf16[4,4,128,128]{3,2,1,0:T(8,128)(2,1)S(1)}, bf16[4,4,128,128]{3,2,1,0:T(8,128)(2,1)S(1)}, u32[]{:S(2)}, u32[]{:S(2)}) collective-permute-start(bf16[4,4,128,128]{3,2,1,0:T(8,128)(2,1)S(1)} %pad_maximum_fusion), channel_id=1, source_target_pairs={{0,128},{128,0},{1,129},{129,1},{2,130},{130,2},{3,131},{131,3},{4... | collective-permute-start | bytes 1572872 | tf_op jit(solution)/shard_map/ppermute | solution.py:262

commit v5 on v4

--- a/solution.py
+++ b/solution.py
@@ -168,7 +168,7 @@
         put(work, 512 * k, 512 * k + 256, (left[256 * k : 256 * k + 256] - dot(diag[256 * k : 256 * k + 256], sol0[theirs])).astype(BF))
     solve(inv, work, sol, piece, (position & 3) * 128)
     stores = []
-    for panel, first, at, count in ((own, depth * 3, 0, 2), (own, depth * 3, 2, 1), (swap, 3 - depth * 3, 0, 2), (swap, 3 - depth * 3, 2, 1)):
+    for panel, first, at, count in ((own, depth * 3, 0, 3), (swap, 3 - depth * 3, 0, 2), (swap, 3 - depth * 3, 2, 1)):
         less(new, state, panel.at[1], first, at, count, sol[...], 0)
         if at == 0:
             @pl.when((position < 8) & (first == 0))

time: 81.4 us -> 81.2 us (level)
  no operation moved by 1% of the time
where the time goes in v5:
time: 81.2 us; the launch traced here: 80.9 us
  blocking collectives  40.8 us (50%)
  Pallas kernels  14.7 us (18%)
  waiting for transfers between devices  11.6 us (14%)
  starting transfers between devices  11.1 us (14%)
  local copies, waits for them, and re-layouts  2.34 us (3%)
    all_to_all x2, blocking collectives, all_to_all(): lax.all_to_all(value, AXES, 0, 0, axis_index_groups=groups, tiled=True)  24.1 us
    all_to_all x1, blocking collectives, per_device(): lax.all_to_all(jnp.broadcast_to(dealt, (8, 96, 128)), 'col', 0, 0, tiled=...  16.7 us
    pallas_call x3, Pallas kernels, call(): pl.pallas_call(body, in_specs=[smem] + [vmem if isinstance(value, list) e...  14.7 us
    ppermute x3, waiting for transfers between devices, per_device(): lax.ppermute(held, AXES, fast_shift(shift))  10.5 us
    ppermute x1, starting transfers between devices, per_device(): lax.ppermute(jnp.stack([part[:, 512:] for part in parts]), 'depth', SWAP)  5.03 us
    ppermute x1, starting transfers between devices, per_device(): swap = lax.ppermute(panels, 'depth', SWAP)  3.24 us
    ppermute x3, starting transfers between devices, per_device(): lax.ppermute(held, AXES, fast_shift(shift))  2.84 us
  transfers between devices with their start and end apart: 5, of which 4 were waited for; matrix products, arithmetic and copies ran while one was open for 3% of the time, Pallas kernels for 11%

profile of v5, /device:TPU:1, one launch (start us, length us, event | category | flops | bytes accessed | tf_op | source)
XLA Modules:
  0.0 80.9 jit_solution(17048270115102318268)
XLA Ops:
  0.0 3.2 %collective-permute-start = (bf16[2,2,3,128,512]{4,3,2,1,0:T(8,128)(2,1)}, bf16[2,2,3,128,512]{4,3,2,1,0:T(8,128)(2,1)S(1)}, u32[]{:S(2)}, u32[]{:S(2)}) collective-permute-start(bf16[2,2,3,128,512]{4,3,2,1,0:T(8,128)(2,1)} %own_ref.1), channel_id=1, source_target_pairs={{0,128},{128,0},{1,129},{129,1},{2,130},{130,2},{3,131},{131,3},{4... | collective-permute-start | bytes 4718600 | tf_op jit(solution)/shard_map/ppermute | solution.py:253
  3.2 0.9 %slice_bitcast_fusion.5 = bf16[128,512]{1,0:T(8,128)(2,1)S(1)} fusion(bf16[2,2,3,128,512]{4,3,2,1,0:T(8,128)(2,1)} %own_ref.1), kind=kLoop, calls=%fused_computation.10 | loop fusion | bytes 262144 | tf_op jit(solution)/shard_map/squeeze | solution.py:254
  4.2 1.1 %slice.60 = bf16[2,1,128,512]{3,2,1,0:T(8,128)(2,1)S(1)} slice(f32[2,6,128,512]{3,2,1,0:T(8,128)} %rhs_ref.1), slice={[0:2], [0:1], [0:128], [0:512]} | slice | bytes 524288 | tf_op jit(solution)/shard_map/slice | solution.py:255
  5.2 0.1 convert_element_type.5
  5.4 1.1 %collective-permute-done.swap_ref = bf16[2,2,3,128,512]{4,3,2,1,0:T(8,128)(2,1)S(1)} collective-permute-done((bf16[2,2,3,128,512]{4,3,2,1,0:T(8,128)(2,1)}, bf16[2,2,3,128,512]{4,3,2,1,0:T(8,128)(2,1)S(1)}, u32[]{:S(2)}, u32[]{:S(2)}) %collective-permute-start) | collective-permute-done | bytes 1572896 | tf_op jit(solution)/shard_map/ppermute | solution.py:253
  6.5 0.0 copy-start
  6.6 14.0 %all_to_all.15 = bf16[16,96,128]{2,1,0:T(8,128)(2,1)S(1)} all-to-all(bf16[16,96,128]{2,1,0:T(8,128)(2,1)S(1)} %pad_maximum_fusion.1), channel_id=1, replica_groups={{0,8,16,24,32,40,48,56,64,72,80,88,96,104,112,120},{1,9,17,25,33,41,49,..., dimensions={0} | all-to-all | bytes 786432 | tf_op jit(solution)/shard_map/all_to_all | solution.py:246
  20.7 16.7 %all_to_all.16 = bf16[8,96,128]{2,1,0:T(8,128)(2,1)S(1)} all-to-all(bf16[8,96,128]{2,1,0:T(8,128)(2,1)S(1)} %broadcast_in_dim.6), channel_id=1, replica_groups=mesh['depth'=2,'row'=16,'col'=8] {'col'}, dimensions={0} | all-to-all | bytes 393216 | tf_op jit(solution)/shard_map/all_to_all | solution.py:258
  37.4 0.1 broadcast_in_dim.7
  37.5 0.0 copy-done
  37.6 10.0 %all_to_all.17.h0 = bf16[4,640,128]{2,1,0:T(8,128)(2,1)S(1)} all-to-all(bf16[4,640,128]{2,1,0:T(8,128)(2,1)S(1)} %broadcast_in_dim.7), channel_id=1, replica_groups={{0,32,64,96},{8,40,72,104},{16,48,80,112},{24,56,88,120},{1,33,65,97},{..., dimensions={0} | all-to-all | bytes 1310720 | tf_op jit(solution)/shard_map/all_to_all | solution.py:246
  47.6 0.7 collective-permute-start.3
  48.3 2.2 %collective-permute-start.2 = (bf16[4,640,128]{2,1,0:T(8,128)(2,1)S(1)}, bf16[4,640,128]{2,1,0:T(8,128)(2,1)S(1)}, u32[]{:S(2)}, u32[]{:S(2)}) collective-permute-start(bf16[4,640,128]{2,1,0:T(8,128)(2,1)S(1)} %all_to_all.17.h0), channel_id=1, source_target_pairs={{0,24},{1,25},{2,26},{3,27},{4,28},{5,29},{6,30},{7,31},{8,0},{9,1... | collective-permute-start | bytes 1966088 | tf_op jit(solution)/shard_map/ppermute | solution.py:261
  50.4 0.1 pad_add_fusion.where_ref
  50.5 0.0 collective-permute-start.1
  50.5 4.8 %shard_map.37 = (bf16[512,1024]{1,0:T(8,128)(2,1)S(1)}, bf16[512,1024]{1,0:T(8,128)(2,1)S(1)}, bf16[2,3,128,1024]{3,2,1,0:T(8,128)(2,1)S(1)}, bf16[2,3,128,1024]...) custom-call(s32[2]{0:T(128)S(1)} %pad_add_fusion.where_ref, ...), custom_call_target="tpu_custom_call" | custom-call | flops 1000000000 | bytes 2500000 | tf_op jit(solution)/shard_map/pallas_call | solution.py:193
  55.3 3.5 %collective-permute-done.3.h3 = bf16[4,640,128]{2,1,0:T(8,128)(2,1)S(1)} collective-permute-done((bf16[4,640,128]{2,1,0:T(8,128)(2,1)S(1)}, bf16[4,640,128]{2,1,0:T(8,128)(2,1)S(1)}, u32[]{:S(2)}, u32[]{:S(2)}) %collective-permute-start.3) | collective-permute-done | bytes 655392 | tf_op jit(solution)/shard_map/ppermute | solution.py:261
  58.8 5.0 %collective-permute-done.2.h2 = bf16[4,640,128]{2,1,0:T(8,128)(2,1)S(1)} collective-permute-done((bf16[4,640,128]{2,1,0:T(8,128)(2,1)S(1)}, bf16[4,640,128]{2,1,0:T(8,128)(2,1)S(1)}, u32[]{:S(2)}, u32[]{:S(2)}) %collective-permute-start.2) | collective-permute-done | bytes 655392 | tf_op jit(solution)/shard_map/ppermute | solution.py:261
  63.9 2.0 %collective-permute-done.1.h1 = bf16[4,640,128]{2,1,0:T(8,128)(2,1)S(1)} collective-permute-done((bf16[4,640,128]{2,1,0:T(8,128)(2,1)S(1)}, bf16[4,640,128]{2,1,0:T(8,128)(2,1)S(1)}, u32[]{:S(2)}, u32[]{:S(2)}) %collective-permute-start.1) | collective-permute-done | bytes 655392 | tf_op jit(solution)/shard_map/ppermute | solution.py:261
  65.9 0.1 pad_maximum_fusion
  65.9 5.0 %collective-permute-start.4 = (bf16[4,4,128,128]{3,2,1,0:T(8,128)(2,1)S(1)}, bf16[4,4,128,128]{3,2,1,0:T(8,128)(2,1)S(1)}, u32[]{:S(2)}, u32[]{:S(2)}) collective-permute-start(bf16[4,4,128,128]{3,2,1,0:T(8,128)(2,1)S(1)} %pad_maximum_fusion), channel_id=1, source_target_pairs={{0,128},{128,0},{1,129},{129,1},{2,130},{130,2},{3,131},{131,3},{4... | collective-permute-start | bytes 1572872 | tf_op jit(solution)/shard_map/ppermute | solution.py:262
  71.0 4.2 %shard_map.38 = (bf16[1024,1024]{1,0:T(8,128)(2,1)S(1)}, f32[4,2,6,128,128]{4,3,2,1,0:T(8,128)S(1)}, f32[512,1024]{1,0:T(8,128)S(1)}) custom-call(s32[2]{0:T(128)S(1)} %pad_add_fusion.where_ref, bf16[4,640,128]{2,1,0:T(8,128)(2,1)S(1)} %all_to_all.17.h0, bf16[4,640,128]{2,1,0:T(8,128)(2,1)S(1)} %collective-permute-done.1.h1, ...), custom_call_target="tpu_custom_call" | custom-call | flops 60000002048 | bytes 150000000 | tf_op jit(solution)/shard_map/pallas_call | solution.py:193
  75.2 0.0 collective-permute-done.4.half
  75.2 5.7 %shard_map.39 = f32[2,6,128,512]{3,2,1,0:T(8,128)} custom-call(s32[2]{0:T(128)S(1)} %pad_add_fusion.where_ref, bf16[1024,1024]{1,0:T(8,128)(2,1)S(1)} %get-tuple-element.21.sol0, f32[4,2,6,128,128]{4,3,2,1,0:T(8,128)S(1)} %get-tuple-element.22.state, f32[512,1024]{1,0:T(8,128)S(1)} %get-tuple-element.23.left, bf16[512,1024]{1,0:T(8,128)(2,1)S(1)} %get-tuple-element.24.inv, ...), custom_call_target="tpu_custom_call" | custom-call | flops 3000000000 | bytes 7500000 | tf_op jit(solution)/shard_map/pallas_call | solution.py:193
  (14 shorter events, 0.2 us)
Async XLA Ops:
  0.0 6.5 %collective-permute-start = (bf16[2,2,3,128,512]{4,3,2,1,0:T(8,128)(2,1)}, bf16[2,2,3,128,512]{4,3,2,1,0:T(8,128)(2,1)S(1)}, u32[]{:S(2)}, u32[]{:S(2)}) collective-permute-start(bf16[2,2,3,128,512]{4,3,2,1,0:T(8,128)(2,1)} %own_ref.1), channel_id=1, source_target_pairs={{0,128},{128,0},{1,129},{129,1},{2,130},{130,2},{3,131},{131,3},{4... | collective-permute-start | bytes 4718600 | tf_op jit(solution)/shard_map/ppermute | solution.py:253
  6.5 31.1 %copy-start = (bf16[2,2,3,128,512]{4,3,2,1,0:T(8,128)(2,1)}, bf16[2,2,3,128,512]{4,3,2,1,0:T(8,128)(2,1)S(1)}, u32[]{:S(2)}) copy-start(bf16[2,2,3,128,512]{4,3,2,1,0:T(8,128)(2,1)S(1)} %collective-permute-done.swap_ref) | copy-start | bytes 4718596
  47.6 11.2 %collective-permute-start.3 = (bf16[4,640,128]{2,1,0:T(8,128)(2,1)S(1)}, bf16[4,640,128]{2,1,0:T(8,128)(2,1)S(1)}, u32[]{:S(2)}, u32[]{:S(2)}) collective-permute-start(bf16[4,640,128]{2,1,0:T(8,128)(2,1)S(1)} %all_to_all.17.h0), channel_id=1, source_target_pairs={{0,16},{1,17},{2,18},{3,19},{4,20},{5,21},{6,22},{7,23},{8,24},{9,... | collective-permute-start | bytes 1966088 | tf_op jit(solution)/shard_map/ppermute | solution.py:261
  48.3 15.6 %collective-permute-start.2 = (bf16[4,640,128]{2,1,0:T(8,128)(2,1)S(1)}, bf16[4,640,128]{2,1,0:T(8,128)(2,1)S(1)}, u32[]{:S(2)}, u32[]{:S(2)}) collective-permute-start(bf16[4,640,128]{2,1,0:T(8,128)(2,1)S(1)} %all_to_all.17.h0), channel_id=1, source_target_pairs={{0,24},{1,25},{2,26},{3,27},{4,28},{5,29},{6,30},{7,31},{8,0},{9,1... | collective-permute-start | bytes 1966088 | tf_op jit(solution)/shard_map/ppermute | solution.py:261
  50.5 15.3 %collective-permute-start.1 = (bf16[4,640,128]{2,1,0:T(8,128)(2,1)S(1)}, bf16[4,640,128]{2,1,0:T(8,128)(2,1)S(1)}, u32[]{:S(2)}, u32[]{:S(2)}) collective-permute-start(bf16[4,640,128]{2,1,0:T(8,128)(2,1)S(1)} %all_to_all.17.h0), channel_id=1, source_target_pairs={{0,8},{1,9},{2,10},{3,11},{4,12},{5,13},{6,14},{7,15},{8,16},{9,17... | collective-permute-start | bytes 1966088 | tf_op jit(solution)/shard_map/ppermute | solution.py:261
  65.9 9.2 %collective-permute-start.4 = (bf16[4,4,128,128]{3,2,1,0:T(8,128)(2,1)S(1)}, bf16[4,4,128,128]{3,2,1,0:T(8,128)(2,1)S(1)}, u32[]{:S(2)}, u32[]{:S(2)}) collective-permute-start(bf16[4,4,128,128]{3,2,1,0:T(8,128)(2,1)S(1)} %pad_maximum_fusion), channel_id=1, source_target_pairs={{0,128},{128,0},{1,129},{129,1},{2,130},{130,2},{3,131},{131,3},{4... | collective-permute-start | bytes 1572872 | tf_op jit(solution)/shard_map/ppermute | solution.py:262

commit v6 on v5

--- a/solution.py
+++ b/solution.py
@@ -123,6 +123,11 @@
     less(state, state, own.at[0], depth * 3, 0, 3, sol[...], 0)
     less(state, state, swap.at[0], 3 - depth * 3, 0, 3, sol[...], 0)
 
+    @pl.when(position < 4)
+    def _():
+        for part in range(2):
+            state[0, part, 0] = piece[:, 128 * part : 128 * part + 128]
+
 
 def lanes(group, shift):
     return pl.ds(pl.multiple_of(((group + 4 - shift) & 3) * 128, 128), 128)
@@ -134,10 +139,10 @@
     for j in range(total.shape[1] // 256):
         for part in range(2):
             place = 256 * j + 128 * part
-            new[tile + j, part, cycles] = old[tile + j, part, cycles] - total[:, place : place + 128].reshape(count, 128, 128)
-
-
-def first_kernel(where_ref, h0, h1, h2, h3, inv0, own, swap, old, known, known_piece, sol, state, left, diag, work, piece):
+            new[tile + j, part, cycles] = (old[tile + j] if isinstance(old, list) else old)[tile + j, part, cycles] - total[:, place : place + 128].reshape(count, 128, 128)
+
+
+def first_kernel(where_ref, h0, h1, h2, h3, inv0, own, swap, old, known, sol, state, left, diag, work, piece):
     depth, position, group, _ = places(where_ref)
     held = (h0, h1, h2, h3)
     for k in range(2):
@@ -148,19 +153,18 @@
     ours = pl.ds(pl.multiple_of(depth * 512, 512), 512)
     for k in range(2):
         left[256 * k : 256 * k + 256] = block(held, 1, k).astype(F32) - dot(diag[256 * k : 256 * k + 256], sol[ours])
-    state[0] = old[0]
     less(state, old, own.at[0], depth * 3, 0, 3, sol[:, 256:], 1)
     less(state, old, swap.at[0], 3 - depth * 3, 0, 3, sol[:, 256:], 1)
 
     @pl.when(position < 4)
     def _():
-        for j in range(TILES):
+        for j in range(1, TILES):
             for part in range(2):
                 at = 256 * j + 128 * part
-                state[j, part, 0] = known_piece[:, at : at + 128] if j == 0 else piece[:, at - 256 : at - 128]
-
-
-def second_kernel(where_ref, sol0, state, left, inv, own, swap, half, out_ref, diag, work, sol, piece, new, out_sems):
+                state[j, part, 0] = piece[:, at - 256 : at - 128]
+
+
+def second_kernel(where_ref, sol0, old, state, left, inv, own, swap, half, out_ref, diag, work, sol, piece, new, out_sems):
     depth, position, group, other_group = places(where_ref)
     fill_diag(diag, [half.at[j] for j in range(TILES)], other_group)
     theirs = pl.ds(pl.multiple_of((1 - depth) * 512, 512), 512)
@@ -169,14 +173,14 @@
     solve(inv, work, sol, piece, (position & 3) * 128)
     stores = []
     for panel, first, at, count in ((own, depth * 3, 0, 3), (swap, 3 - depth * 3, 0, 2), (swap, 3 - depth * 3, 2, 1)):
-        less(new, state, panel.at[1], first, at, count, sol[...], 0)
+        less(new, [old] + [state] * (TILES - 1), panel.at[1], first, at, count, sol[...], 0)
         if at == 0:
             @pl.when((position < 8) & (first == 0))
             def _():
                 for j in range(TILES):
                     for part in range(2):
                         place = 256 * j + 128 * part
-                        new[j, part, 0] = jnp.where(position < 4, state[j, part, 0], piece[:, place : place + 128])
+                        new[j, part, 0] = jnp.where(position < 4, (state if j else old)[j, part, 0], piece[:, place : place + 128])
 
         cycles = pl.ds(first + at, count)
         stores += fill([(new.at[j, :, cycles], out_ref.at[:, cycles, :, lanes(group, shift)]) for j, shift in enumerate(SHIFTS)], out_sems, len(stores))
@@ -203,7 +207,7 @@
     inverses, own, swap, rhs = [pltpu.with_memory_space_constraint(value, pltpu.HBM) for value in (inverses, own, swap, rhs)]
     inverse, half = pltpu.VMEM((512, 1024), BF), pltpu.VMEM((2, 3, 128, 1024), BF)
     state = pltpu.VMEM((TILES, 2, 6, 128, 128), F32)
-    inv0, inv1, own, swap, old, known, piece = call(
+    inv0, inv1, own, swap, old, known, _ = call(
         load_kernel,
         1_000_000_000,
         [inverse, inverse, half, half, state, pltpu.VMEM((1024, 256), BF), pltpu.VMEM((128, 256), F32)],
@@ -223,7 +227,7 @@
             pltpu.VMEM((1024, 768), BF),
             pltpu.VMEM((128, 768), F32),
         ],
-        *[[value] for value in (*held, inv0, own, swap, old, known, piece)],
+        *[[value] for value in (*held, inv0, own, swap, old, known)],
     )
     (out,) = call(
         second_kernel,
@@ -237,7 +241,7 @@
             state,
             pltpu.SemaphoreType.DMA((16,)),
         ],
-        *[[value] for value in (sol, new, left, inv1, own, swap, other)],
+        *[[value] for value in (sol, old, new, left, inv1, own, swap, other)],
     )
     return out
 

time: 81.2 us -> 81.1 us (level)
  transfers between devices with their start and end apart: 5 -> 5, of which waited for: 4 -> 4; matrix products, arithmetic and copies ran while one was open for 3% -> 3% of each run, Pallas kernels for 11% -> 12%
where the time goes in v6:
time: 81.1 us; the launch traced here: 80.9 us
  blocking collectives  40.8 us (50%)
  Pallas kernels  15.3 us (19%)
  starting transfers between devices  11.1 us (14%)
  waiting for transfers between devices  11 us (14%)
  local copies, waits for them, and re-layouts  2.34 us (3%)
    all_to_all x2, blocking collectives, all_to_all(): lax.all_to_all(value, AXES, 0, 0, axis_index_groups=groups, tiled=True)  24.1 us
    all_to_all x1, blocking collectives, per_device(): lax.all_to_all(jnp.broadcast_to(dealt, (8, 96, 128)), 'col', 0, 0, tiled=...  16.7 us
    pallas_call x3, Pallas kernels, call(): pl.pallas_call(body, in_specs=[smem] + [vmem if isinstance(value, list) e...  15.3 us
    ppermute x3, waiting for transfers between devices, per_device(): lax.ppermute(held, AXES, fast_shift(shift))  9.86 us
    ppermute x1, starting transfers between devices, per_device(): lax.ppermute(jnp.stack([part[:, 512:] for part in parts]), 'depth', SWAP)  5.03 us
    ppermute x1, starting transfers between devices, per_device(): swap = lax.ppermute(panels, 'depth', SWAP)  3.24 us
    ppermute x3, starting transfers between devices, per_device(): lax.ppermute(held, AXES, fast_shift(shift))  2.84 us
  transfers between devices with their start and end apart: 5, of which 4 were waited for; matrix products, arithmetic and copies ran while one was open for 3% of the time, Pallas kernels for 12%

profile of v6, /device:TPU:1, one launch (start us, length us, event | category | flops | bytes accessed | tf_op | source)
XLA Modules:
  0.0 80.9 jit_solution(4171458043914143582)
XLA Ops:
  0.0 3.2 %collective-permute-start = (bf16[2,2,3,128,512]{4,3,2,1,0:T(8,128)(2,1)}, bf16[2,2,3,128,512]{4,3,2,1,0:T(8,128)(2,1)S(1)}, u32[]{:S(2)}, u32[]{:S(2)}) collective-permute-start(bf16[2,2,3,128,512]{4,3,2,1,0:T(8,128)(2,1)} %own_ref.1), channel_id=1, source_target_pairs={{0,128},{128,0},{1,129},{129,1},{2,130},{130,2},{3,131},{131,3},{4... | collective-permute-start | bytes 4718600 | tf_op jit(solution)/shard_map/ppermute | solution.py:257
  3.2 0.9 %slice_bitcast_fusion.5 = bf16[128,512]{1,0:T(8,128)(2,1)S(1)} fusion(bf16[2,2,3,128,512]{4,3,2,1,0:T(8,128)(2,1)} %own_ref.1), kind=kLoop, calls=%fused_computation.10 | loop fusion | bytes 262144 | tf_op jit(solution)/shard_map/squeeze | solution.py:258
  4.2 1.1 %slice.60 = bf16[2,1,128,512]{3,2,1,0:T(8,128)(2,1)S(1)} slice(f32[2,6,128,512]{3,2,1,0:T(8,128)} %rhs_ref.1), slice={[0:2], [0:1], [0:128], [0:512]} | slice | bytes 524288 | tf_op jit(solution)/shard_map/slice | solution.py:259
  5.2 0.1 convert_element_type.5
  5.4 1.1 %collective-permute-done.swap_ref = bf16[2,2,3,128,512]{4,3,2,1,0:T(8,128)(2,1)S(1)} collective-permute-done((bf16[2,2,3,128,512]{4,3,2,1,0:T(8,128)(2,1)}, bf16[2,2,3,128,512]{4,3,2,1,0:T(8,128)(2,1)S(1)}, u32[]{:S(2)}, u32[]{:S(2)}) %collective-permute-start) | collective-permute-done | bytes 1572896 | tf_op jit(solution)/shard_map/ppermute | solution.py:257
  6.5 0.0 copy-start
  6.6 14.0 %all_to_all.15 = bf16[16,96,128]{2,1,0:T(8,128)(2,1)S(1)} all-to-all(bf16[16,96,128]{2,1,0:T(8,128)(2,1)S(1)} %pad_maximum_fusion.1), channel_id=1, replica_groups={{0,8,16,24,32,40,48,56,64,72,80,88,96,104,112,120},{1,9,17,25,33,41,49,..., dimensions={0} | all-to-all | bytes 786432 | tf_op jit(solution)/shard_map/all_to_all | solution.py:250
  20.7 16.7 %all_to_all.16 = bf16[8,96,128]{2,1,0:T(8,128)(2,1)S(1)} all-to-all(bf16[8,96,128]{2,1,0:T(8,128)(2,1)S(1)} %broadcast_in_dim.6), channel_id=1, replica_groups=mesh['depth'=2,'row'=16,'col'=8] {'col'}, dimensions={0} | all-to-all | bytes 393216 | tf_op jit(solution)/shard_map/all_to_all | solution.py:262
  37.4 0.1 broadcast_in_dim.7
  37.5 0.0 copy-done
  37.6 10.0 %all_to_all.17.h0 = bf16[4,640,128]{2,1,0:T(8,128)(2,1)S(1)} all-to-all(bf16[4,640,128]{2,1,0:T(8,128)(2,1)S(1)} %broadcast_in_dim.7), channel_id=1, replica_groups={{0,32,64,96},{8,40,72,104},{16,48,80,112},{24,56,88,120},{1,33,65,97},{..., dimensions={0} | all-to-all | bytes 1310720 | tf_op jit(solution)/shard_map/all_to_all | solution.py:250
  47.6 0.7 collective-permute-start.3
  48.3 2.2 %collective-permute-start.2 = (bf16[4,640,128]{2,1,0:T(8,128)(2,1)S(1)}, bf16[4,640,128]{2,1,0:T(8,128)(2,1)S(1)}, u32[]{:S(2)}, u32[]{:S(2)}) collective-permute-start(bf16[4,640,128]{2,1,0:T(8,128)(2,1)S(1)} %all_to_all.17.h0), channel_id=1, source_target_pairs={{0,24},{1,25},{2,26},{3,27},{4,28},{5,29},{6,30},{7,31},{8,0},{9,1... | collective-permute-start | bytes 1966088 | tf_op jit(solution)/shard_map/ppermute | solution.py:265
  50.4 0.1 pad_add_fusion.where_ref
  50.5 0.0 collective-permute-start.1
  50.5 5.4 %shard_map.37 = (bf16[512,1024]{1,0:T(8,128)(2,1)S(1)}, bf16[512,1024]{1,0:T(8,128)(2,1)S(1)}, bf16[2,3,128,1024]{3,2,1,0:T(8,128)(2,1)S(1)}, bf16[2,3,128,1024]...) custom-call(s32[2]{0:T(128)S(1)} %pad_add_fusion.where_ref, ...), custom_call_target="tpu_custom_call" | custom-call | flops 1000000000 | bytes 2500000 | tf_op jit(solution)/shard_map/pallas_call | solution.py:197
  56.0 2.9 %collective-permute-done.3.h3 = bf16[4,640,128]{2,1,0:T(8,128)(2,1)S(1)} collective-permute-done((bf16[4,640,128]{2,1,0:T(8,128)(2,1)S(1)}, bf16[4,640,128]{2,1,0:T(8,128)(2,1)S(1)}, u32[]{:S(2)}, u32[]{:S(2)}) %collective-permute-start.3) | collective-permute-done | bytes 655392 | tf_op jit(solution)/shard_map/ppermute | solution.py:265
  58.8 5.0 %collective-permute-done.2.h2 = bf16[4,640,128]{2,1,0:T(8,128)(2,1)S(1)} collective-permute-done((bf16[4,640,128]{2,1,0:T(8,128)(2,1)S(1)}, bf16[4,640,128]{2,1,0:T(8,128)(2,1)S(1)}, u32[]{:S(2)}, u32[]{:S(2)}) %collective-permute-start.2) | collective-permute-done | bytes 655392 | tf_op jit(solution)/shard_map/ppermute | solution.py:265
  63.9 2.0 %collective-permute-done.1.h1 = bf16[4,640,128]{2,1,0:T(8,128)(2,1)S(1)} collective-permute-done((bf16[4,640,128]{2,1,0:T(8,128)(2,1)S(1)}, bf16[4,640,128]{2,1,0:T(8,128)(2,1)S(1)}, u32[]{:S(2)}, u32[]{:S(2)}) %collective-permute-start.1) | collective-permute-done | bytes 655392 | tf_op jit(solution)/shard_map/ppermute | solution.py:265
  65.9 0.1 pad_maximum_fusion
  65.9 5.0 %collective-permute-start.4 = (bf16[4,4,128,128]{3,2,1,0:T(8,128)(2,1)S(1)}, bf16[4,4,128,128]{3,2,1,0:T(8,128)(2,1)S(1)}, u32[]{:S(2)}, u32[]{:S(2)}) collective-permute-start(bf16[4,4,128,128]{3,2,1,0:T(8,128)(2,1)S(1)} %pad_maximum_fusion), channel_id=1, source_target_pairs={{0,128},{128,0},{1,129},{129,1},{2,130},{130,2},{3,131},{131,3},{4... | collective-permute-start | bytes 1572872 | tf_op jit(solution)/shard_map/ppermute | solution.py:266
  71.0 4.1 %shard_map.38 = (bf16[1024,1024]{1,0:T(8,128)(2,1)S(1)}, f32[4,2,6,128,128]{4,3,2,1,0:T(8,128)S(1)}, f32[512,1024]{1,0:T(8,128)S(1)}) custom-call(s32[2]{0:T(128)S(1)} %pad_add_fusion.where_ref, bf16[4,640,128]{2,1,0:T(8,128)(2,1)S(1)} %all_to_all.17.h0, bf16[4,640,128]{2,1,0:T(8,128)(2,1)S(1)} %collective-permute-done.1.h1, ...), custom_call_target="tpu_custom_call" | custom-call | flops 60000002048 | bytes 150000000 | tf_op jit(solution)/shard_map/pallas_call | solution.py:197
  75.1 0.0 collective-permute-done.4.half
  75.1 5.7 %shard_map.39 = f32[2,6,128,512]{3,2,1,0:T(8,128)} custom-call(s32[2]{0:T(128)S(1)} %pad_add_fusion.where_ref, bf16[1024,1024]{1,0:T(8,128)(2,1)S(1)} %get-tuple-element.19.sol0, f32[4,2,6,128,128]{4,3,2,1,0:T(8,128)S(1)} %get-tuple-element.17.old, f32[4,2,6,128,128]{4,3,2,1,0:T(8,128)S(1)} %get-tuple-element.20.state, ...), custom_call_target="tpu_custom_call" | custom-call | flops 3000000000 | bytes 7500000 | tf_op jit(solution)/shard_map/pallas_call | solution.py:197
  (14 shorter events, 0.2 us)
Async XLA Ops:
  0.0 6.5 %collective-permute-start = (bf16[2,2,3,128,512]{4,3,2,1,0:T(8,128)(2,1)}, bf16[2,2,3,128,512]{4,3,2,1,0:T(8,128)(2,1)S(1)}, u32[]{:S(2)}, u32[]{:S(2)}) collective-permute-start(bf16[2,2,3,128,512]{4,3,2,1,0:T(8,128)(2,1)} %own_ref.1), channel_id=1, source_target_pairs={{0,128},{128,0},{1,129},{129,1},{2,130},{130,2},{3,131},{131,3},{4... | collective-permute-start | bytes 4718600 | tf_op jit(solution)/shard_map/ppermute | solution.py:257
  6.5 31.1 %copy-start = (bf16[2,2,3,128,512]{4,3,2,1,0:T(8,128)(2,1)}, bf16[2,2,3,128,512]{4,3,2,1,0:T(8,128)(2,1)S(1)}, u32[]{:S(2)}) copy-start(bf16[2,2,3,128,512]{4,3,2,1,0:T(8,128)(2,1)S(1)} %collective-permute-done.swap_ref) | copy-start | bytes 4718596
  47.6 11.2 %collective-permute-start.3 = (bf16[4,640,128]{2,1,0:T(8,128)(2,1)S(1)}, bf16[4,640,128]{2,1,0:T(8,128)(2,1)S(1)}, u32[]{:S(2)}, u32[]{:S(2)}) collective-permute-start(bf16[4,640,128]{2,1,0:T(8,128)(2,1)S(1)} %all_to_all.17.h0), channel_id=1, source_target_pairs={{0,16},{1,17},{2,18},{3,19},{4,20},{5,21},{6,22},{7,23},{8,24},{9,... | collective-permute-start | bytes 1966088 | tf_op jit(solution)/shard_map/ppermute | solution.py:265
  48.3 15.6 %collective-permute-start.2 = (bf16[4,640,128]{2,1,0:T(8,128)(2,1)S(1)}, bf16[4,640,128]{2,1,0:T(8,128)(2,1)S(1)}, u32[]{:S(2)}, u32[]{:S(2)}) collective-permute-start(bf16[4,640,128]{2,1,0:T(8,128)(2,1)S(1)} %all_to_all.17.h0), channel_id=1, source_target_pairs={{0,24},{1,25},{2,26},{3,27},{4,28},{5,29},{6,30},{7,31},{8,0},{9,1... | collective-permute-start | bytes 1966088 | tf_op jit(solution)/shard_map/ppermute | solution.py:265
  50.5 15.3 %collective-permute-start.1 = (bf16[4,640,128]{2,1,0:T(8,128)(2,1)S(1)}, bf16[4,640,128]{2,1,0:T(8,128)(2,1)S(1)}, u32[]{:S(2)}, u32[]{:S(2)}) collective-permute-start(bf16[4,640,128]{2,1,0:T(8,128)(2,1)S(1)} %all_to_all.17.h0), channel_id=1, source_target_pairs={{0,8},{1,9},{2,10},{3,11},{4,12},{5,13},{6,14},{7,15},{8,16},{9,17... | collective-permute-start | bytes 1966088 | tf_op jit(solution)/shard_map/ppermute | solution.py:265
  65.9 9.2 %collective-permute-start.4 = (bf16[4,4,128,128]{3,2,1,0:T(8,128)(2,1)S(1)}, bf16[4,4,128,128]{3,2,1,0:T(8,128)(2,1)S(1)}, u32[]{:S(2)}, u32[]{:S(2)}) collective-permute-start(bf16[4,4,128,128]{3,2,1,0:T(8,128)(2,1)S(1)} %pad_maximum_fusion), channel_id=1, source_target_pairs={{0,128},{128,0},{1,129},{129,1},{2,130},{130,2},{3,131},{131,3},{4... | collective-permute-start | bytes 1572872 | tf_op jit(solution)/shard_map/ppermute | solution.py:266
